TPU v7x, 256 devices: a whole 4x4x8 slice. The times are simulated.
256 devices in a mesh: frame: 16 (over y, x_hi, core), patch: 16 (over x_lo, z).
Axes of the slice: x: 4 (x_hi: 2, x_lo: 2; x = x_hi * 2 + x_lo), y: 4, z: 8, core: 2. Of those that a mesh axis runs over, the one named last changes fastest.
Arguments:
- hidden_states: bfloat16 [16, 4096, 1152], P('frame', 'patch'), may hold values from -6 to 6
- modulation: float32 [6, 1152], replicated, may hold values from -0.5 to 1.5
- w_qkv_spatial: bfloat16 [1152, 3456], P('frame'), as said below
- w_out_spatial: bfloat16 [1152, 1152], P('frame'), may hold values from -0.1875 to 0.1875
- w_qkv_temporal: bfloat16 [1152, 3456], P('frame'), as said below
- w_out_temporal: bfloat16 [1152, 1152], P('frame'), may hold values from -0.1875 to 0.1875
Outputs:
- block_out: bfloat16 [16, 4096, 1152], P('frame', 'patch')
Inputs may be any that keep to these rules, and one draw needn't show every extreme that they name: `w_qkv_spatial`: an ordinary projection of 1152 inputs to 3456 outputs. `w_qkv_temporal`: an ordinary projection of 1152 inputs to 3456 outputs.
All inputs are finite; a program needn't handle non-finite values.
Results may differ from a plain program's by a relative error of at most 0.02.
Values may be sent and summed in bfloat16 or wider, within the bound.
A program may use at most 128 MiB of HBM per device.

v0:
```python
import math

import jax
import jax.numpy as jnp
from jax import lax
from jax.sharding import PartitionSpec as P

HEAD_SIZE = 72


def layer_norm(value_rows):
    value_rows = value_rows.astype(jnp.float32)
    centred = value_rows - jnp.mean(value_rows, axis=-1, keepdims=True)
    variance = jnp.mean(centred * centred, axis=-1, keepdims=True)
    return centred * lax.rsqrt(variance + 1e-06)


def modulate(value_rows, shift, scale):
    return (layer_norm(value_rows) * (1.0 + scale) + shift).astype(jnp.bfloat16)


def flatten(value_rows):
    return value_rows.reshape(value_rows.shape[0] * value_rows.shape[1], value_rows.shape[2])


def heads_first(value_rows):
    frames, patches, inner = value_rows.shape
    split = value_rows.reshape(frames, patches, inner // HEAD_SIZE, HEAD_SIZE)
    return split.transpose(2, 1, 0, 3)


def empty_state(query_rows):
    heads, batch, count, size = query_rows.shape
    return (
        jnp.full((heads, batch, count), -1e30, jnp.float32),
        jnp.zeros((heads, batch, count), jnp.float32),
        jnp.zeros((heads, batch, count, size), jnp.float32),
    )


def head_step(items):
    running, total, accum, query_rows, key_rows, value_rows = items
    attention_scores = jnp.einsum(
        "pim,pom->pio", query_rows, key_rows, preferred_element_type=jnp.float32
    ) * HEAD_SIZE ** (-0.5)
    newmax = jnp.maximum(running, jnp.max(attention_scores, axis=-1))
    factor = jnp.exp(running - newmax)
    attention_probabilities = jnp.exp(attention_scores - newmax[..., None])
    total = total * factor + jnp.sum(attention_probabilities, axis=-1)
    update = jnp.einsum(
        "pog,pga->poa",
        attention_probabilities.astype(jnp.bfloat16),
        value_rows,
        preferred_element_type=jnp.float32,
    )
    return (newmax, total, accum * factor[..., None] + update)


def fold_heads(state, query_rows, key_rows, value_rows):
    return lax.map(head_step, (state[0], state[1], state[2], query_rows, key_rows, value_rows))


def finish(state):
    out = state[2] / state[1][..., None]
    heads, batch, count, size = out.shape
    out = out.transpose(2, 1, 0, 3)
    return out.reshape(out.shape[0], out.shape[1], heads * size).astype(jnp.bfloat16)


def spatial_local(parts):
    query_rows = parts[:, :, 0].transpose(2, 0, 1, 3)
    key_rows = parts[:, :, 1].transpose(2, 0, 1, 3)
    value_rows = parts[:, :, 2].transpose(2, 0, 1, 3)
    heads, frames, count, size = query_rows.shape
    block = math.gcd(count, 512)
    block_list = count // block
    grouped = query_rows.reshape(heads, frames, block_list, block, size).transpose(2, 0, 1, 3, 4)

    def one_block(query_block):
        state = fold_heads(empty_state(query_block), query_block, key_rows, value_rows)
        return state[2] / state[1][..., None]

    out = lax.map(one_block, grouped)
    out = out.transpose(2, 0, 3, 1, 4).reshape(frames, count, heads, size)
    return out.astype(jnp.bfloat16)


def temporal_local(parts):
    frames_all, single_group, items, inner = parts[0].shape
    shaped = [p.reshape(frames_all, items, inner) for p in parts]
    query_loc = heads_first(shaped[0])
    state_loc = fold_heads(
        empty_state(query_loc), query_loc, heads_first(shaped[1]), heads_first(shaped[2])
    )
    return finish(state_loc).reshape(frames_all, single_group, items, inner)


def body(hidden_states, modulation, w_qkv_spatial, w_out_spatial, w_qkv_temporal, w_out_temporal):
    inner = w_qkv_spatial.shape[1] // 3
    frames, patches, width = hidden_states.shape
    full_qkv_s, full_out_s, full_qkv_t, full_out_t = (
        lax.all_gather(w_qkv_spatial, "frame", axis=0, tiled=True),
        lax.all_gather(w_out_spatial, "frame", axis=0, tiled=True),
        lax.all_gather(w_qkv_temporal, "frame", axis=0, tiled=True),
        lax.all_gather(w_out_temporal, "frame", axis=0, tiled=True),
    )
    normed_s = modulate(hidden_states, modulation[0], modulation[1])
    qkv_flat = jnp.dot(flatten(normed_s), full_qkv_s, preferred_element_type=jnp.float32)
    qkv_s = qkv_flat.astype(jnp.bfloat16).reshape(frames, patches, 3 * inner)
    stacked = qkv_s.reshape(frames, patches, 3, inner // HEAD_SIZE, HEAD_SIZE)
    spread = spatial_local(
        lax.all_to_all(stacked, "patch", split_axis=3, concat_axis=1, tiled=True)
    )
    spatial_attention_output = lax.all_to_all(
        spread, "patch", split_axis=1, concat_axis=2, tiled=True
    ).reshape(frames, patches, inner)
    proj_s = jnp.dot(
        flatten(spatial_attention_output), full_out_s, preferred_element_type=jnp.float32
    )
    middle = (
        hidden_states.astype(jnp.float32) + modulation[2] * proj_s.reshape(frames, patches, width)
    ).astype(jnp.bfloat16)
    normed_t = modulate(middle, modulation[3], modulation[4])
    qkv_flat_t = jnp.dot(flatten(normed_t), full_qkv_t, preferred_element_type=jnp.float32)
    qkv_t = qkv_flat_t.astype(jnp.bfloat16).reshape(frames, patches, 3 * inner)
    query_t = qkv_t[..., :inner]
    keys_t = qkv_t[..., inner : 2 * inner]
    values_t = qkv_t[..., 2 * inner :]
    groups = lax.axis_size("frame")
    per_group = patches // groups
    grouped_q = query_t.reshape(frames, groups, per_group, inner)
    grouped_k = keys_t.reshape(frames, groups, per_group, inner)
    grouped_v = values_t.reshape(frames, groups, per_group, inner)
    spread_t = temporal_local(
        (
            lax.all_to_all(grouped_q, "frame", split_axis=1, concat_axis=0, tiled=True),
            lax.all_to_all(grouped_k, "frame", split_axis=1, concat_axis=0, tiled=True),
            lax.all_to_all(grouped_v, "frame", split_axis=1, concat_axis=0, tiled=True),
        )
    )
    attn_t = lax.all_to_all(spread_t, "frame", split_axis=0, concat_axis=1, tiled=True).reshape(
        frames, patches, inner
    )
    proj_t = jnp.dot(flatten(attn_t), full_out_t, preferred_element_type=jnp.float32)
    return (
        middle.astype(jnp.float32) + modulation[5] * proj_t.reshape(frames, patches, width)
    ).astype(jnp.bfloat16)


def solution(mesh):
    in_specs = (
        P("frame", "patch", None),
        P(),
        P("frame", None),
        P("frame", None),
        P("frame", None),
        P("frame", None),
    )
    out_specs = P("frame", "patch", None)
    return jax.shard_map(body, mesh=mesh, in_specs=in_specs, out_specs=out_specs, check_vma=False)
```

profile of v0, /device:TPU:1, one launch (start us, length us, event | category | flops | bytes accessed | tf_op | source)
XLA Modules:
  0.0 379.0 jit_solution(9150759802881417577)
XLA Ops:
  8.0 1.8 slice_reduce_fusion.1
  9.8 1.2 convert_reduce_fusion
  11.0 1.4 fusion.48
  12.4 78.1 %all-gather.5.cloned.1.call-done = bf16[1152,3456]{1,0:T(8,128)(2,1)} async-done(((bf16[72,3456]{1,0:T(8,128)(2,1)}), bf16[1152,3456]{1,0:T(8,128)(2,1)}) %all-gather.5.cloned.1.call-update) | async-done | bytes 7962640 | tf_op jit(solution)/shard_map/all_gather | solution.py:102
  90.5 6.0 %convolution_convert_fusion.1 = bf16[256,3456]{1,0:T(8,128)(2,1)S(1)} fusion(bf16[1152,3456]{1,0:T(8,128)(2,1)} %all-gather.5.cloned.1.call-done, bf16[1,256,1152]{2,1,0:T(8,128)(2,1)S(1)} %copy-done, f32[1152]{0:T(1024)S(1)} %get-tuple-element.115, f32[1152]{0:T(1024)S(1)} %get-tuple-element.116, f32[256]{0:T(256)S(1)} %add_rsqrt_fusion.1, ...), kind=kOutput, calls=%fused_computation.39 | convolution fusion | flops 2041085952 | bytes 10333184 | tf_op jit(solution)/shard_map/dot_general | solution.py:108
  97.4 1.3 copy.31
  98.7 6.8 %all-to-all-start = ((bf16[1,256,3,16,72]{1,4,2,0,3:T(8,128)(2,1)}), bf16[1,256,3,16,72]{1,4,2,0,3:T(8,128)(2,1)S(1)}, u32[]{:S(2)}, u32[]{:S(2)}) async-start(bf16[1,256,3,16,72]{1,4,2,0,3:T(8,128)(2,1)} %copy.31), calls=%async_computation | async-start | bytes 3538944 | tf_op jit(solution)/shard_map/all_to_all | solution.py:112
  106.3 40.8 %all-to-all-done = bf16[1,256,3,16,72]{1,4,2,0,3:T(8,128)(2,1)S(1)} async-done(((bf16[1,256,3,16,72]{1,4,2,0,3:T(8,128)(2,1)}), bf16[1,256,3,16,72]{1,4,2,0,3:T(8,128)(2,1)S(1)}, u32[]{:S(2)}, u32[]{:S(2)}) %all-to-all-start) | async-done | bytes 1769504 | tf_op jit(solution)/shard_map/all_to_all | solution.py:112
  149.6 1.5 copy.35
  151.2 42.2 %while.18 = (s32[]{:T(128)}, bf16[8,1,1,512,72]{3,4,2,1,0:T(8,128)(2,1)}, bf16[8,1,1,512,72]{4,3,2,1,0:T(8,128)(2,1)S(1)}, bf16[1,1,4096,72]{3,2,1,0:T(8,128)(2,...) while((s32[]{:T(128)}, bf16[8,1,1,512,72]{3,4,2,1,0:T(8,128)(2,1)}, ...), condition=%wide.region_5.6_spmd, body=%wide.region_2.5_spmd.sunk | while | flops 620832256 | bytes 27107912 | solution.py:83
  151.2 1.3 multiply_reduce_fusion.3
  152.5 1.5 fusion.85
  154.1 2.4 fusion.86
  156.5 1.3 multiply_reduce_fusion.3
  157.8 1.5 fusion.85
  159.3 2.4 fusion.86
  161.7 1.3 multiply_reduce_fusion.3
  163.1 1.5 fusion.85
  164.6 2.4 fusion.86
  167.0 1.3 multiply_reduce_fusion.3
  168.3 1.5 fusion.85
  169.9 2.4 fusion.86
  172.3 1.3 multiply_reduce_fusion.3
  173.6 1.5 fusion.85
  175.1 2.4 fusion.86
  177.5 1.3 multiply_reduce_fusion.3
  178.9 1.5 fusion.85
  180.4 2.4 fusion.86
  182.8 1.3 multiply_reduce_fusion.3
  184.1 1.5 fusion.85
  185.7 2.4 fusion.86
  188.1 1.3 multiply_reduce_fusion.3
  189.4 1.5 fusion.85
  190.9 2.4 fusion.86
  193.3 1.5 copy.50
  195.9 22.6 %reduce.20 = bf16[4096,72]{1,0:T(8,128)(2,1)S(1)} reduce(bf16[4096,1,1,72]{3,2,1,0:T(2,128)(2,1)S(1)} %bitcast.139, bf16[]{:T(256)} %broadcast.226), dimensions={1,2}, to_apply=%bitcast.105.reduce_sub_computation | reduce | bytes 1179650
  218.5 2.1 reshape.266
  220.6 23.5 %all_to_all.69 = bf16[16,2,9216]{2,1,0:T(2,128)(2,1)S(1)} all-to-all(bf16[16,2,9216]{2,1,0:T(2,128)(2,1)S(1)} %reshape.266), channel_id=1, replica_groups=mesh['frame'=16,'patch'=16] {'patch'}, dimensions={0} | all-to-all | bytes 1179648 | tf_op jit(solution)/shard_map/all_to_all | solution.py:114
  244.2 3.6 reshape.267
  247.8 2.3 copy.38
  251.2 2.9 fusion.67
  254.4 5.9 %fusion.38 = bf16[1,256,3456]{2,1,0:T(8,128)(2,1)S(1)} fusion(bf16[1152,3456]{1,0:T(8,128)(2,1)} %all-gather.9.cloned.1.call-done, f32[1,256,1152]{2,1,0:T(8,128)S(1)} %get-tuple-element.157, f32[1152]{0:T(1024)S(1)} %get-tuple-element.118, f32[1152]{0:T(1024)S(1)} %copy-done.2, f32[256]{0:T(256)S(1)} %add_rsqrt_fusion, f32[256]{0:T(256)S(1)} %broadcast_multiply_fusion), kind=kOutput, calls=%fused_computation.40 | convolution fusion | flops 2040791040 | bytes 10923008 | tf_op jit(solution)/shard_map/dot_general | solution.py:124
  261.3 19.6 %all_to_all.70 = bf16[1,16,16,1152]{3,2,0,1:T(8,128)(2,1)} all-to-all(bf16[1,16,16,1152]{3,2,0,1:T(8,128)(2,1)S(1)} %bitcast.150), channel_id=1, replica_groups=mesh['frame'=16,'patch'=16] {'frame'}, dimensions={1} | all-to-all | bytes 1179648 | tf_op jit(solution)/shard_map/all_to_all | solution.py:136
  280.9 15.6 %all_to_all.71 = bf16[1,16,16,1152]{3,2,0,1:T(8,128)(2,1)S(1)} all-to-all(bf16[1,16,16,1152]{3,2,0,1:T(8,128)(2,1)S(1)} %bitcast.149), channel_id=1, replica_groups=mesh['frame'=16,'patch'=16] {'frame'}, dimensions={1} | all-to-all | bytes 1179648 | tf_op jit(solution)/shard_map/all_to_all | solution.py:137
  296.5 3.8 %all-to-all-start.4 = ((bf16[1,16,16,1152]{3,2,0,1:T(8,128)(2,1)}), bf16[1,16,16,1152]{3,2,0,1:T(8,128)(2,1)S(1)}, u32[]{:S(2)}, u32[]{:S(2)}) async-start(bf16[1,16,16,1152]{3,2,0,1:T(8,128)(2,1)} %bitcast.28), calls=%async_computation.4 | async-start | bytes 1179648 | tf_op jit(solution)/shard_map/all_to_all | solution.py:138
  300.9 3.2 reshape_reshape.20
  304.2 1.7 copy.43
  305.9 1.8 reshape_reshape.21
  307.7 1.7 copy.44
  309.4 3.0 all-to-all-done.4
  312.4 1.8 reshape_reshape.22
  315.0 32.5 %while.28 = (s32[]{:T(128)}, f32[16,16,16]{2,1,0:T(8,128)S(1)}, f32[16,16,16,72]{3,2,1,0:T(8,128)}, bf16[16,16,16,72]{3,2,1,0:T(8,128)(2,1)}, bf16[16,16,16,72]{...) while((s32[]{:T(128)}, f32[16,16,16]{2,1,0:T(8,128)S(1)}, ...), condition=%wide.region_11.12_spmd, body=%wide.region_8.11_spmd.sunk | while | flops 1223938 | bytes 540753 | solution.py:60
  315.0 1.0 fusion.89
  317.0 1.0 fusion.89
  319.0 1.0 fusion.89
  321.1 1.0 fusion.89
  323.1 1.0 fusion.89
  325.1 1.0 fusion.89
  327.2 1.0 fusion.89
  347.5 2.0 fusion.52
  350.1 2.1 convert_element_type.75
  352.2 4.6 %all-to-all-start.5 = ((bf16[16,1,16,1152]{3,2,1,0:T(8,128)(2,1)}), bf16[16,1,16,1152]{3,2,1,0:T(8,128)(2,1)S(1)}, u32[]{:S(2)}, u32[]{:S(2)}) async-start(bf16[16,1,16,1152]{3,2,1,0:T(8,128)(2,1)} %bitcast.31), calls=%async_computation.5 | async-start | bytes 1179648 | tf_op jit(solution)/shard_map/all_to_all | solution.py:141
  356.9 12.1 %all-to-all-done.5 = bf16[16,1,16,1152]{3,2,1,0:T(8,128)(2,1)S(1)} async-done(((bf16[16,1,16,1152]{3,2,1,0:T(8,128)(2,1)}), bf16[16,1,16,1152]{3,2,1,0:T(8,128)(2,1)S(1)}, u32[]{:S(2)}, u32[]{:S(2)}) %all-to-all-start.5) | async-done | bytes 589856 | tf_op jit(solution)/shard_map/all_to_all | solution.py:141
  368.9 3.6 fusion.43
  (128 shorter events, 35.4 us)
Async XLA Ops:
  6.5 84.0 %copy-start = (bf16[1,256,1152]{2,1,0:T(8,128)(2,1)S(1)}, bf16[1,256,1152]{2,1,0:T(8,128)(2,1)}, u32[]{:S(2)}) copy-start(bf16[1,256,1152]{2,1,0:T(8,128)(2,1)} %param.10) | copy-start | bytes 1769476
  6.5 84.0 %all-gather.5.cloned.1.call-start = ((), (), s32[]{:S(2)}) async-start(), calls=%async_computation.6 | async-start | bytes 8460288 | tf_op jit(solution)/shard_map/all_gather | solution.py:102
  7.3 243.2 %all-gather.7.cloned.1.call-start = ((), (), s32[]{:S(2)}) async-start(), calls=%async_computation.7 | async-start | bytes 2820096 | tf_op jit(solution)/shard_map/all_gather | solution.py:103
  98.7 48.4 %all-to-all-start = ((bf16[1,256,3,16,72]{1,4,2,0,3:T(8,128)(2,1)}), bf16[1,256,3,16,72]{1,4,2,0,3:T(8,128)(2,1)S(1)}, u32[]{:S(2)}, u32[]{:S(2)}) async-start(bf16[1,256,3,16,72]{1,4,2,0,3:T(8,128)(2,1)} %copy.31), calls=%async_computation | async-start | bytes 3538944 | tf_op jit(solution)/shard_map/all_to_all | solution.py:112
  105.6 148.8 %all-gather.9.cloned.1.call-start = ((), (), s32[]{:S(2)}) async-start(), calls=%async_computation.8 | async-start | bytes 8460288 | tf_op jit(solution)/shard_map/all_gather | solution.py:104
  250.1 1.1 copy-start.1
  250.1 1.1 copy-start.3
  251.2 3.2 copy-start.2
  296.5 15.9 %all-to-all-start.4 = ((bf16[1,16,16,1152]{3,2,0,1:T(8,128)(2,1)}), bf16[1,16,16,1152]{3,2,0,1:T(8,128)(2,1)S(1)}, u32[]{:S(2)}, u32[]{:S(2)}) async-start(bf16[1,16,16,1152]{3,2,0,1:T(8,128)(2,1)} %bitcast.28), calls=%async_computation.4 | async-start | bytes 1179648 | tf_op jit(solution)/shard_map/all_to_all | solution.py:138
  300.4 56.5 %all-gather.11.cloned.1.call-start = ((), (), s32[]{:S(2)}) async-start(), calls=%async_computation.9 | async-start | bytes 2820096 | tf_op jit(solution)/shard_map/all_gather | solution.py:105
  352.2 16.7 %all-to-all-start.5 = ((bf16[16,1,16,1152]{3,2,1,0:T(8,128)(2,1)}), bf16[16,1,16,1152]{3,2,1,0:T(8,128)(2,1)S(1)}, u32[]{:S(2)}, u32[]{:S(2)}) async-start(bf16[16,1,16,1152]{3,2,1,0:T(8,128)(2,1)} %bitcast.31), calls=%async_computation.5 | async-start | bytes 1179648 | tf_op jit(solution)/shard_map/all_to_all | solution.py:141
Sparse Core Ops, SparseCore 0:
  10.0 80.4 all-gather.4
  93.2 59.6 all-gather.6
  155.5 78.5 all-gather.8
  303.6 51.3 all-gather.10
where the time goes:
time: 381 us; the launch traced here: 379 us
  waiting for transfers between devices  137 us (36%)
  matrix products  79.1 us (21%)
  blocking collectives  58.7 us (15%)
  other arithmetic  42.5 us (11%)
  local copies, waits for them, and re-layouts  32.5 us (9%)
  starting transfers between devices  15.5 us (4%)
  between operations  13.4 us (4%)
    all_gather x1, waiting for transfers between devices, body(): lax.all_gather(w_qkv_spatial, 'frame', axis=0, tiled=True)  78.1 us
    all_to_all x1, waiting for transfers between devices, body(): lax.all_to_all(stacked, 'patch', split_axis=3, concat_axis=1, tiled=True)  40.8 us
    dot_general x24, matrix products, head_step(): jnp.einsum('pog,pga->poa', attention_probabilities.astype(jnp.bfloat16),...  33.3 us
    dot_general x24, matrix products, head_step(): jnp.einsum('pim,pom->pio', query_rows, key_rows, preferred_element_type=j...  27.4 us
    all_to_all x1, blocking collectives, body(): lax.all_to_all(spread, 'patch', split_axis=1, concat_axis=2, tiled=True)  23.5 us
    unnamed x1, other arithmetic  22.6 us
    all_to_all x1, blocking collectives, body(): lax.all_to_all(grouped_q, 'frame', split_axis=1, concat_axis=0, tiled=True)  19.6 us
    all_to_all x1, blocking collectives, body(): lax.all_to_all(grouped_k, 'frame', split_axis=1, concat_axis=0, tiled=True)  15.6 us
  transfers between devices with their start and end apart: 7, of which 4 were waited for; matrix products, arithmetic and copies ran while one was open for 38% of the time, Pallas kernels for 0%

commit v1 on v0

v1 whole, which is shorter than its diff:
```python
import math

import jax
import jax.numpy as jnp
from jax import lax
from jax.experimental import pallas as pl
from jax.experimental.pallas import tpu as pltpu
from jax.sharding import PartitionSpec as P

HEAD = 72
HEADS = 16
D = 1152
TOK = 256
ROWS = 80
HALF = 2944
Q_SCALE = HEAD ** (-0.5) * math.log2(math.e)
F32 = jnp.float32
BF16 = jnp.bfloat16


def remote(src, dst, send, recv, frame, patch):
    return pltpu.make_async_remote_copy(
        src_ref=src,
        dst_ref=dst,
        send_sem=send,
        recv_sem=recv,
        device_id={"frame": frame, "patch": patch},
        device_id_type=pl.DeviceIdType.MESH,
    )


def signal(sem, frame, patch):
    pl.semaphore_signal(
        sem, inc=1, device_id={"frame": frame, "patch": patch}, device_id_type=pl.DeviceIdType.MESH
    )


def norm_modulate(x, shift, scale):
    centred = x - jnp.mean(x, axis=-1, keepdims=True)
    variance = jnp.mean(centred * centred, axis=-1, keepdims=True)
    return centred * lax.rsqrt(variance + 1e-06) * (1.0 + scale) + shift


def spatial_kernel(
    hid, mod, wsel, wrest, attn, wfull,
    nz, wsel_all, wc, qkv, stage, kn, ostage, w1, w2,
    zs, zr, ss, sr, xs, xr, os, orr, ws, wr,
):
    f = lax.axis_index("frame")
    p = lax.axis_index("patch")
    core = lax.rem(f, 2)
    x_hi = lax.rem(f // 2, 2)
    y = f // 4
    x_lo = p // 8
    z = lax.rem(p, 8)
    chip = f // 2
    other_core = f + 1 - 2 * core
    cross_f = (y * 2 + 1 - x_hi) * 2 + core
    cross_p = (1 - x_lo) * 8 + z
    x_pair = (1 - x_lo) * 8 + z
    y_up = lax.rem(y + 1, 4) * 4 + x_hi * 2 + core
    y_dn = lax.rem(y + 3, 4) * 4 + x_hi * 2 + core
    z_up = x_lo * 8 + lax.rem(z + 1, 8)
    z_dn = x_lo * 8 + lax.rem(z + 7, 8)

    barrier = pltpu.get_barrier_semaphore()

    def greet(i, c):
        signal(barrier, lax.rem(f + i, 16), p)
        signal(barrier, f, lax.rem(p + i, 16))
        return c

    lax.fori_loop(1, 16, greet, 0)
    signal(barrier, cross_f, cross_p)
    pl.semaphore_wait(barrier, 31)

    def send_sel(i, c):
        peer = lax.rem(f + i, 16)
        remote(wsel, wsel_all.at[f], ss.at[i], sr.at[f], peer, p).start()
        return c

    lax.fori_loop(1, 16, send_sel, 0)
    first = remote(wrest.at[1 - core], w1, ws.at[0], wr.at[0], other_core, p)
    first.start()

    nz[z] = norm_modulate(hid[...].astype(F32), mod[0:1], mod[1:2]).astype(BF16)

    def z_copy(step, way, sub):
        at = lax.rem(z + 8 - step, 8) if way == 0 else lax.rem(z + step, 8)
        block = nz.at[at, pl.ds(128 * sub, 128)]
        n = (step * 2 + way) * 2 + sub
        return remote(block, block, zs.at[n], zr.at[n], f, z_up if way == 0 else z_dn)

    def z_arrival(step, way, sub):
        at = lax.rem(z + 7 - step, 8) if way == 0 else lax.rem(z + step + 1, 8)
        block = nz.at[at, pl.ds(128 * sub, 128)]
        n = (step * 2 + way) * 2 + sub
        return remote(block, block, zs.at[n], zr.at[n], f, z_up if way == 0 else z_dn)

    def sends(step, way, sub):
        return step < 3 or sub == way

    for sub in range(2):
        for way in range(2):
            z_copy(0, way, sub).start()

    first.wait()
    mine = wrest[core, 0:72, :].astype(F32)
    theirs = w1[0:72, :].astype(F32)
    is_first = core == 0
    low = jnp.where(is_first, mine, theirs)
    high = jnp.where(is_first, theirs, mine)
    w2[...] = jnp.concatenate([low, high], axis=0).astype(BF16)

    def rows144(n):
        return wfull.at[core, pl.ds(pl.multiple_of(144 * n, 144), 144)]

    keep = pltpu.make_async_copy(w2, rows144(chip), ws.at[1])
    keep.start()
    across = remote(w2, rows144(chip), ws.at[2], wr.at[2], cross_f, cross_p)
    across.start()
    across_in = remote(w2, rows144(2 * y + 1 - x_hi), ws.at[2], wr.at[2], cross_f, cross_p)

    y_prev = lax.rem(y + 3, 4)
    y_next = lax.rem(y + 1, 4)
    y_far = lax.rem(y + 2, 4)

    def y_send(way, sub):
        n = 3 + way * 2 + sub
        block = rows144(2 * y + sub)
        return remote(block, block, ws.at[n], wr.at[n], y_up if way == 0 else y_dn, p)

    def y_in(way, sub):
        n = 3 + way * 2 + sub
        block = rows144(2 * (y_prev if way == 0 else y_next) + sub)
        return remote(block, block, ws.at[n], wr.at[n], y_up if way == 0 else y_dn, p)

    def y_pass(way):
        block = rows144(2 * (y_prev if way == 0 else y_next) + way)
        return remote(block, block, ws.at[7 + way], wr.at[7 + way], y_up if way == 0 else y_dn, p)

    def y_pass_in(way):
        block = rows144(2 * y_far + way)
        return remote(block, block, ws.at[7 + way], wr.at[7 + way], y_up if way == 0 else y_dn, p)

    def core_send(n):
        block = rows144(n)
        return remote(block, block, ws.at[9 + n], wr.at[9 + n], other_core, p)

    def core_in(n):
        block = wfull.at[1 - core, pl.ds(pl.multiple_of(144 * n, 144), 144)]
        return remote(block, block, ws.at[9 + n], wr.at[9 + n], other_core, p)

    zero8 = jnp.zeros((8, TOK), F32)
    ones8 = jnp.where(lax.broadcasted_iota(jnp.int32, (8, TOK), 0) == 0, 1.0, 0.0)

    def to_natural(slot):
        kt = qkv[slot, ROWS : 2 * ROWS, :].astype(F32)
        kt = jnp.concatenate([kt, jnp.zeros((128 - ROWS, TOK), F32)], axis=0)
        kn[pl.ds(pl.multiple_of(slot * TOK, TOK), TOK), :] = kt.T.astype(BF16)

    def pair_copy(at, n):
        slot = qkv.at[x_lo * 8 + at]
        return remote(stage.at[n], slot, xs.at[n], xr.at[n], f, x_pair)

    def pair_in(at, n):
        slot = qkv.at[(1 - x_lo) * 8 + at]
        return remote(stage.at[n], slot, xs.at[n], xr.at[n], f, x_pair)

    def project(at, n):
        r = jnp.dot(nz[at], wc[...], preferred_element_type=F32)
        t = r.T
        own = [t[0:72] * Q_SCALE, zero8, t[144:216], zero8, t[288:360], ones8]
        oth = [t[72:144] * Q_SCALE, zero8, t[216:288], zero8, t[360:432], ones8]
        stage[n] = jnp.concatenate(oth, axis=0).astype(BF16)
        pair_copy(at, n).start()
        qkv[x_lo * 8 + at] = jnp.concatenate(own, axis=0).astype(BF16)
        to_natural(x_lo * 8 + at)

    def z_forward(step):
        for sub in range(2):
            for way in range(2):
                if sends(step, way, sub):
                    z_arrival(step, way, sub).wait_recv()
                    if step < 3 and sends(step + 1, way, sub):
                        z_copy(step + 1, way, sub).start()

    z_forward(0)

    def take_sel(i, c):
        peer = lax.rem(f + i, 16)
        remote(wsel, wsel_all.at[peer], ss.at[i], sr.at[peer], peer, p).wait()
        return c

    wsel_all[f] = wsel[...]
    lax.fori_loop(1, 16, take_sel, 0)
    for j in range(8):
        a = wsel_all[2 * j, 0:72, :].astype(F32)
        b = wsel_all[2 * j + 1, 0:72, :].astype(F32)
        wc[144 * j : 144 * j + 144, :] = jnp.concatenate([a, b], axis=0).astype(BF16)

    project(z, 0)
    project(lax.rem(z + 7, 8), 1)
    project(lax.rem(z + 1, 8), 2)
    z_forward(1)
    keep.wait()
    across_in.wait()
    for sub in range(2):
        for way in range(2):
            y_send(way, sub).start()
    core_send(2 * y).start()
    core_send(2 * y + 1).start()
    project(lax.rem(z + 6, 8), 3)
    project(lax.rem(z + 2, 8), 4)
    z_forward(2)
    project(lax.rem(z + 5, 8), 5)
    project(lax.rem(z + 3, 8), 6)
    z_forward(3)
    project(lax.rem(z + 4, 8), 7)
    for step in range(4):
        for way in range(2):
            for sub in range(2):
                if sends(step, way, sub):
                    z_copy(step, way, sub).wait_send()
    order = [0, 7, 1, 6, 2, 5, 3, 4]
    for n in range(8):
        at = lax.rem(z + order[n], 8)
        pair_copy(at, n).wait_send()
        pair_in(at, n).wait_recv()
        to_natural((1 - x_lo) * 8 + at)

    head = 2 * z + x_lo
    KB = 512

    def attend(i, c):
        dest = lax.rem(p + 1 + i, 16)
        q_t = qkv[dest, 0:ROWS, :]
        top = None
        for kb in range(4096 // KB):
            s = jnp.dot(
                kn[kb * KB : (kb + 1) * KB, 0:ROWS], q_t, preferred_element_type=F32
            )
            new = jnp.max(s, axis=0, keepdims=True)
            if top is not None:
                new = jnp.maximum(top, new)
            prob = jnp.exp2(s - new).astype(BF16)
            part = None
            for u in range(KB // TOK):
                v_t = qkv[kb * (KB // TOK) + u, 2 * ROWS : 3 * ROWS, :]
                o = jnp.dot(v_t, prob[u * TOK : (u + 1) * TOK], preferred_element_type=F32)
                part = o if part is None else part + o
            acc = part if top is None else acc * jnp.exp2(top - new) + part
            top = new
        out = acc[0:HEAD] / acc[HEAD : HEAD + 1]
        ostage[i] = jnp.concatenate([out, zero8], axis=0).astype(BF16)

        @pl.when(i < 15)
        def _():
            remote(ostage.at[i], attn.at[head], os.at[i], orr.at[head], f, dest).start()

        @pl.when(i == 15)
        def _():
            attn[head] = ostage[i]

        return c

    lax.fori_loop(0, 5, attend, 0)
    y_in(0, 0).wait_recv()
    y_pass(0).start()
    core_send(2 * y_prev).start()
    y_in(1, 0).wait_recv()
    core_send(2 * y_next).start()
    lax.fori_loop(5, 11, attend, 0)
    y_in(1, 1).wait_recv()
    y_pass(1).start()
    core_send(2 * y_next + 1).start()
    y_in(0, 1).wait_recv()
    core_send(2 * y_prev + 1).start()
    lax.fori_loop(11, 16, attend, 0)

    y_pass_in(0).wait_recv()
    core_send(2 * y_far).start()
    y_pass_in(1).wait_recv()
    core_send(2 * y_far + 1).start()

    def finish(i, c):
        dest = lax.rem(p + 1 + i, 16)
        src_head = 2 * lax.rem(dest, 8) + dest // 8
        remote(ostage.at[i], attn.at[head], os.at[i], orr.at[head], f, dest).wait_send()
        remote(ostage.at[i], attn.at[src_head], os.at[i], orr.at[src_head], f, dest).wait_recv()
        return c

    lax.fori_loop(0, 15, finish, 0)
    for way in range(2):
        for sub in range(2):
            y_send(way, sub).wait_send()
        y_pass(way).wait_send()
    for n in range(8):
        core_send(n).wait_send()
        core_in(n).wait_recv()


def temporal_kernel(
    hid, mod, attn, wfull, out,
    w, at32, mid, midt, proj, qkv, acc, osend,
    wsem, ms, mr, bs, br,
):
    f = lax.axis_index("frame")
    p = lax.axis_index("patch")
    load0 = pltpu.make_async_copy(wfull.at[0], w.at[0], wsem.at[0])
    load1 = pltpu.make_async_copy(wfull.at[1], w.at[1], wsem.at[1])
    load0.start()
    load1.start()
    barrier = pltpu.get_barrier_semaphore()

    def greet(i, c):
        signal(barrier, lax.rem(f + i, 16), p)
        return c

    lax.fori_loop(1, 16, greet, 0)

    for h in range(HEADS):
        at32[HEAD * h : HEAD * h + HEAD, :] = attn[h, 0:HEAD, :].astype(F32)
    for j in range(9):
        proj[:, 128 * j : 128 * j + 128] = at32[128 * j : 128 * j + 128, :].T.astype(BF16)
    load0.wait()
    r = jnp.dot(proj[...], w[0, :, 0:D], preferred_element_type=F32)
    mid[...] = (hid[...].astype(F32) + mod[2:3] * r).astype(BF16)
    pl.semaphore_wait(barrier, 15)

    def rows16(ref, n):
        return ref.at[pl.ds(pl.multiple_of(16 * n, 16), 16)]

    def send_mid(i, c):
        peer = lax.rem(f + i, 16)
        remote(rows16(mid, peer), rows16(midt, f), ms.at[i], mr.at[f], peer, p).start()
        return c

    lax.fori_loop(1, 16, send_mid, 0)
    here = pl.ds(pl.multiple_of(16 * f, 16), 16)
    midt[here, :] = mid[here, :]
    load1.wait()

    def take_mid(i, c):
        peer = lax.rem(f + i, 16)
        remote(rows16(mid, peer), rows16(midt, peer), ms.at[i], mr.at[peer], peer, p).wait()
        return c

    lax.fori_loop(1, 16, take_mid, 0)
    proj[...] = norm_modulate(midt[...].astype(F32), mod[3:4], mod[4:5]).astype(BF16)
    a = jnp.dot(proj[...], w[0, :, D:HALF], preferred_element_type=F32)
    qkv[:, 0:D] = (a[:, 0:D] * Q_SCALE).astype(BF16)
    qkv[:, D : HALF - D] = a[:, D:].astype(BF16)
    b = jnp.dot(proj[...], w[1, :, 0 : 4 * D - HALF], preferred_element_type=F32)
    qkv[:, HALF - D : 3 * D] = b.astype(BF16)

    ri = lax.broadcasted_iota(jnp.int32, (TOK, TOK), 0)
    ci = lax.broadcasted_iota(jnp.int32, (TOK, TOK), 1)
    same = lax.rem(ri, 16) == lax.rem(ci, 16)
    lane = lax.broadcasted_iota(jnp.int32, (TOK, TOK), 1)
    acc[...] = jnp.zeros_like(acc)
    for h in range(HEADS):
        start = 128 * min(HEAD * h // 128, 7)
        low = HEAD * h - start
        inside = (lane >= low) & (lane < low + HEAD)
        q = qkv[:, start : start + 256]
        q = jnp.where(inside, q, jnp.zeros_like(q))
        k = qkv[:, D + start : D + start + 256]
        v = qkv[:, 2 * D + start : 2 * D + start + 256]
        s = lax.dot_general(q, k, (((1,), (1,)), ((), ())), preferred_element_type=F32)
        s = jnp.where(same, s, -1e30)
        prob = jnp.exp2(s - jnp.max(s, axis=1, keepdims=True))
        total = jnp.sum(prob, axis=1, keepdims=True)
        o = jnp.dot(prob.astype(BF16), v, preferred_element_type=F32) / total
        acc[:, start : start + 256] = jnp.where(inside, o, acc[:, start : start + 256])
    r = jnp.dot(
        acc[...].astype(BF16), w[1, :, 4 * D - HALF : 5 * D - HALF], preferred_element_type=F32
    )
    osend[...] = (midt[...].astype(F32) + mod[5:6] * r).astype(BF16)

    def send_out(i, c):
        peer = lax.rem(f + i, 16)
        remote(rows16(osend, peer), rows16(out, f), bs.at[i], br.at[f], peer, p).start()
        return c

    lax.fori_loop(1, 16, send_out, 0)
    out[here, :] = osend[here, :]

    def take_out(i, c):
        peer = lax.rem(f + i, 16)
        remote(rows16(osend, peer), rows16(out, peer), bs.at[i], br.at[peer], peer, p).wait()
        return c

    lax.fori_loop(1, 16, take_out, 0)


VMEM = pl.BlockSpec(memory_space=pltpu.VMEM)
ANY = pl.BlockSpec(memory_space=pl.ANY)
LIMIT = 60 * 1024 * 1024


def spatial_call(hid, mod, wsel, wrest):
    dma = pltpu.SemaphoreType.DMA
    return pl.pallas_call(
        spatial_kernel,
        out_shape=(
            jax.ShapeDtypeStruct((HEADS, ROWS, TOK), BF16),
            jax.ShapeDtypeStruct((2, D, HALF), BF16),
        ),
        in_specs=[VMEM] * 4,
        out_specs=(VMEM, ANY),
        scratch_shapes=[
            pltpu.VMEM((8, TOK, D), BF16),
            pltpu.VMEM((16, ROWS, 512), BF16),
            pltpu.VMEM((D, 512), BF16),
            pltpu.VMEM((16, 3 * ROWS, TOK), BF16),
            pltpu.VMEM((8, 3 * ROWS, TOK), BF16),
            pltpu.VMEM((4096, 128), BF16),
            pltpu.VMEM((16, ROWS, TOK), BF16),
            pltpu.VMEM((ROWS, HALF), BF16),
            pltpu.VMEM((144, HALF), BF16),
            dma((16,)), dma((16,)),
            dma((16,)), dma((16,)),
            dma((8,)), dma((8,)),
            dma((16,)), dma((16,)),
            dma((17,)), dma((17,)),
        ],
        compiler_params=pltpu.CompilerParams(
            collective_id=0, has_side_effects=True, vmem_limit_bytes=LIMIT
        ),
        name="spatial",
    )(hid, mod, wsel, wrest)


def temporal_call(hid, mod, attn, wfull):
    dma = pltpu.SemaphoreType.DMA
    return pl.pallas_call(
        temporal_kernel,
        out_shape=jax.ShapeDtypeStruct((TOK, D), BF16),
        in_specs=[VMEM, VMEM, VMEM, ANY],
        out_specs=VMEM,
        scratch_shapes=[
            pltpu.VMEM((2, D, HALF), BF16),
            pltpu.VMEM((D, TOK), F32),
            pltpu.VMEM((TOK, D), BF16),
            pltpu.VMEM((TOK, D), BF16),
            pltpu.VMEM((TOK, D), BF16),
            pltpu.VMEM((TOK, 3 * D), BF16),
            pltpu.VMEM((TOK, D), F32),
            pltpu.VMEM((TOK, D), BF16),
            dma((2,)),
            dma((16,)), dma((16,)),
            dma((16,)), dma((16,)),
        ],
        compiler_params=pltpu.CompilerParams(
            collective_id=1, has_side_effects=True, vmem_limit_bytes=LIMIT
        ),
        name="temporal",
    )(hid, mod, attn, wfull)


def body(hidden_states, modulation, w_qkv_spatial, w_out_spatial, w_qkv_temporal, w_out_temporal):
    p = lax.axis_index("patch")
    x_lo, z = p // 8, lax.rem(p, 8)
    hid = hidden_states.reshape(TOK, D)
    heads = w_qkv_spatial.reshape(HEAD, 3, HEADS, HEAD)
    own = lax.dynamic_slice_in_dim(heads, 2 * z + x_lo, 1, axis=2)
    other = lax.dynamic_slice_in_dim(heads, 2 * z + 1 - x_lo, 1, axis=2)
    wsel = jnp.concatenate([own, other], axis=2).reshape(HEAD, 6 * HEAD)
    wsel = jnp.pad(wsel, ((0, ROWS - HEAD), (0, 512 - 6 * HEAD)))
    rest = jnp.concatenate([w_out_spatial, w_qkv_temporal, w_out_temporal], axis=1)
    rest = jnp.pad(rest, ((0, ROWS - HEAD), (0, 2 * HALF - 5 * D)))
    rest = jnp.stack([rest[:, :HALF], rest[:, HALF:]])
    attn, wfull = spatial_call(hid, modulation, wsel, rest)
    out = temporal_call(hid, modulation, attn, wfull)
    return out.reshape(1, TOK, D)


def solution(mesh):
    in_specs = (
        P("frame", "patch", None),
        P(),
        P("frame", None),
        P("frame", None),
        P("frame", None),
        P("frame", None),
    )
    out_specs = P("frame", "patch", None)
    return jax.shard_map(body, mesh=mesh, in_specs=in_specs, out_specs=out_specs, check_vma=False)
```

time: 381 us -> 164 us (0.43)
  Pallas kernels: 0 us -> 157 us
  waiting for transfers between devices: 137 us -> 0 us
  matrix products: 79.1 us -> 0 us
  blocking collectives: 58.7 us -> 0 us
  other arithmetic: 42.5 us -> 1.41 us
  local copies, waits for them, and re-layouts: 32.5 us -> 5.78 us
  starting transfers between devices: 15.5 us -> 0 us
  between operations: 13.4 us -> 0.09 us
    pallas_call x0 -> x2, Pallas kernels: none -> 157 us  [the longest x1 126 us: spatial_call(): pl.pallas_call(spatial_kernel, out_shape=(jax.ShapeDtypeStruct((HEADS, RO...]
    dot_general x52 -> x0, matrix products: 79.1 us -> none  [the longest x24 33.3 us: head_step(): jnp.einsum('pog,pga->poa', attention_probabilities.astype(jnp.bfloat16),...]
    all_gather x4 -> x0, waiting for transfers between devices: 78.2 us -> none  [the longest x1 78.1 us: body(): lax.all_gather(w_qkv_spatial, 'frame', axis=0, tiled=True)]
    all_to_all x3 -> x0, blocking collectives: 58.7 us -> none  [the longest x1 23.5 us: body(): lax.all_to_all(spread, 'patch', split_axis=1, concat_axis=2, tiled=True)]
    all_to_all x3 -> x0, waiting for transfers between devices: 55.9 us -> none  [the longest x1 40.8 us: body(): lax.all_to_all(stacked, 'patch', split_axis=3, concat_axis=1, tiled=True)]
    unnamed x1 -> x0, other arithmetic: 22.6 us -> none
    reduce_sum x27 -> x0, other arithmetic: 15.6 us -> none  [the longest x24 12.8 us: head_step(): total = total * factor + jnp.sum(attention_probabilities, axis=-1)]
    all_to_all x3 -> x0, starting transfers between devices: 15.2 us -> none  [the longest x1 6.85 us: body(): lax.all_to_all(stacked, 'patch', split_axis=3, concat_axis=1, tiled=True)]
  transfers between devices with their start and end apart: 7 -> 0, of which waited for: 4 -> 0; matrix products, arithmetic and copies ran while one was open for 38% -> 0% of each run, Pallas kernels for 0% -> 0%
where the time goes in v1:
time: 164 us
  Pallas kernels  157 us (96%)
  local copies, waits for them, and re-layouts  5.78 us (4%)
    pallas_call x1, Pallas kernels, spatial_call(): pl.pallas_call(spatial_kernel, out_shape=(jax.ShapeDtypeStruct((HEADS, RO...  126 us
    pallas_call x1, Pallas kernels, temporal_call(): pl.pallas_call(temporal_kernel, out_shape=jax.ShapeDtypeStruct((TOK, D),...  31 us

profile of v1, /device:TPU:1, one launch (start us, length us, event | category | flops | bytes accessed | tf_op | source)
XLA Modules:
  0.0 164.1 jit_solution(121474517023277774)
XLA Ops:
  0.0 0.0 copy-start.1
  0.0 0.0 copy-start
  0.0 0.0 copy-start.2
  0.0 2.8 %reshape.13 = bf16[72,3,16,72]{3,2,1,0:T(8,128)(2,1)S(1)} reshape(bf16[72,3456]{1,0:T(8,128)(2,1)} %param.8) | data formatting | bytes 995328 | tf_op jit(solution)/shard_map/reshape | solution.py:466
  2.8 0.2 constant_dynamic-slice_fusion.1
  3.1 0.3 pad_maximum_fusion.1
  3.4 0.1 reshape.14
  3.5 0.6 pad.8.wsel
  4.1 0.0 copy-done.1
  4.1 0.0 copy-done
  4.1 0.0 copy-done.2
  4.1 0.1 fusion.8
  4.2 0.1 slice_bitcast_fusion.1
  4.3 1.0 pad_maximum_fusion.wrest
  5.3 125.8 %spatial.1 = (bf16[16,80,256]{2,1,0:T(8,128)(2,1)}, bf16[2,1152,2944]{2,1,0:T(8,128)(2,1)}) custom-call(bf16[256,1152]{1,0:T(8,128)(2,1)} %bitcast.6, f32[6,1152]{1,0:T(8,128)} %mod.3, bf16[80,512]{1,0:T(8,128)(2,1)} %pad.8.wsel, bf16[2,80,2944]{2,1,0:T(8,128)(2,1)} %pad_maximum_fusion.wrest), custom_call_target="tpu_custom_call" | custom-call | tf_op jit(solution)/shard_map/spatial/pallas_call | solution.py:404
  131.1 31.0 %temporal.1 = bf16[256,1152]{1,0:T(8,128)(2,1)} custom-call(bf16[256,1152]{1,0:T(8,128)(2,1)} %bitcast.7, f32[6,1152]{1,0:T(8,128)} %mod.3, bf16[16,80,256]{2,1,0:T(8,128)(2,1)} %get-tuple-element.7.attn, bf16[2,1152,2944]{2,1,0:T(8,128)(2,1)} %get-tuple-element.8.wfull), custom_call_target="tpu_custom_call" | custom-call | tf_op jit(solution)/shard_map/temporal/pallas_call | solution.py:437
  162.2 1.9 %copy.8 = bf16[1,256,1152]{2,1,0:T(8,128)(2,1)} copy(bf16[1,256,1152]{2,1,0:T(8,128)(2,1)} %bitcast.8) | data formatting | bytes 1179648
Async XLA Ops:
  0.0 4.1 %copy-start.1 = (bf16[72,1152]{1,0:T(8,128)(2,1)S(1)}, bf16[72,1152]{1,0:T(8,128)(2,1)}, u32[]{:S(2)}) copy-start(bf16[72,1152]{1,0:T(8,128)(2,1)} %param.11) | copy-start | bytes 497668
  0.0 4.1 %copy-start = (bf16[72,3456]{1,0:T(8,128)(2,1)S(1)}, bf16[72,3456]{1,0:T(8,128)(2,1)}, u32[]{:S(2)}) copy-start(bf16[72,3456]{1,0:T(8,128)(2,1)} %param.10) | copy-start | bytes 1492996
  0.0 4.1 %copy-start.2 = (bf16[72,1152]{1,0:T(8,128)(2,1)S(1)}, bf16[72,1152]{1,0:T(8,128)(2,1)}, u32[]{:S(2)}) copy-start(bf16[72,1152]{1,0:T(8,128)(2,1)} %param.9) | copy-start | bytes 497668

commit v2 on v1

--- a/solution.py
+++ b/solution.py
@@ -43,7 +43,7 @@
 
 def spatial_kernel(
     hid, mod, wsel, wrest, attn, wfull,
-    nz, wsel_all, wc, qkv, stage, kn, ostage, w1, w2,
+    nz, wsel_all, wc, qkv, stage, kn, ostage, w1, w2, score_a, score_b, top_a, top_b, top_all, acc_all,
     zs, zr, ss, sr, xs, xr, os, orr, ws, wr,
 ):
     f = lax.axis_index("frame")
@@ -72,18 +72,8 @@
 
     lax.fori_loop(1, 16, greet, 0)
     signal(barrier, cross_f, cross_p)
+    nz[z] = norm_modulate(hid[...].astype(F32), mod[0:1], mod[1:2]).astype(BF16)
     pl.semaphore_wait(barrier, 31)
-
-    def send_sel(i, c):
-        peer = lax.rem(f + i, 16)
-        remote(wsel, wsel_all.at[f], ss.at[i], sr.at[f], peer, p).start()
-        return c
-
-    lax.fori_loop(1, 16, send_sel, 0)
-    first = remote(wrest.at[1 - core], w1, ws.at[0], wr.at[0], other_core, p)
-    first.start()
-
-    nz[z] = norm_modulate(hid[...].astype(F32), mod[0:1], mod[1:2]).astype(BF16)
 
     def z_copy(step, way, sub):
         at = lax.rem(z + 8 - step, 8) if way == 0 else lax.rem(z + step, 8)
@@ -103,6 +93,16 @@
     for sub in range(2):
         for way in range(2):
             z_copy(0, way, sub).start()
+
+    first = remote(wrest.at[1 - core], w1, ws.at[0], wr.at[0], other_core, p)
+    first.start()
+
+    def send_sel(i, c):
+        peer = lax.rem(f + i, 16)
+        remote(wsel, wsel_all.at[f], ss.at[i], sr.at[f], peer, p).start()
+        return c
+
+    lax.fori_loop(1, 16, send_sel, 0)
 
     first.wait()
     mine = wrest[core, 0:72, :].astype(F32)
@@ -112,6 +112,9 @@
     high = jnp.where(is_first, theirs, mine)
     w2[...] = jnp.concatenate([low, high], axis=0).astype(BF16)
 
+    def chip_of(at_y, kind):
+        return 2 * at_y + (x_hi if kind == 0 else 1 - x_hi)
+
     def rows144(n):
         return wfull.at[core, pl.ds(pl.multiple_of(144 * n, 144), 144)]
 
@@ -119,31 +122,33 @@
     keep.start()
     across = remote(w2, rows144(chip), ws.at[2], wr.at[2], cross_f, cross_p)
     across.start()
-    across_in = remote(w2, rows144(2 * y + 1 - x_hi), ws.at[2], wr.at[2], cross_f, cross_p)
+    across_in = remote(w2, rows144(chip_of(y, 1)), ws.at[2], wr.at[2], cross_f, cross_p)
 
     y_prev = lax.rem(y + 3, 4)
     y_next = lax.rem(y + 1, 4)
     y_far = lax.rem(y + 2, 4)
 
-    def y_send(way, sub):
-        n = 3 + way * 2 + sub
-        block = rows144(2 * y + sub)
+    def y_send(way, kind):
+        n = 3 + way * 2 + kind
+        block = rows144(chip_of(y, kind))
+        source = w2 if kind == 0 else block
+        return remote(source, block, ws.at[n], wr.at[n], y_up if way == 0 else y_dn, p)
+
+    def y_in(way, kind):
+        n = 3 + way * 2 + kind
+        block = rows144(chip_of(y_prev if way == 0 else y_next, kind))
         return remote(block, block, ws.at[n], wr.at[n], y_up if way == 0 else y_dn, p)
 
-    def y_in(way, sub):
-        n = 3 + way * 2 + sub
-        block = rows144(2 * (y_prev if way == 0 else y_next) + sub)
-        return remote(block, block, ws.at[n], wr.at[n], y_up if way == 0 else y_dn, p)
-
     def y_pass(way):
-        block = rows144(2 * (y_prev if way == 0 else y_next) + way)
+        block = rows144(chip_of(y_prev if way == 0 else y_next, way))
         return remote(block, block, ws.at[7 + way], wr.at[7 + way], y_up if way == 0 else y_dn, p)
 
     def y_pass_in(way):
-        block = rows144(2 * y_far + way)
+        block = rows144(chip_of(y_far, way))
         return remote(block, block, ws.at[7 + way], wr.at[7 + way], y_up if way == 0 else y_dn, p)
 
-    def core_send(n):
+    def core_send(at_y, kind):
+        n = chip_of(at_y, kind)
         block = rows144(n)
         return remote(block, block, ws.at[9 + n], wr.at[9 + n], other_core, p)
 
@@ -151,31 +156,45 @@
         block = wfull.at[1 - core, pl.ds(pl.multiple_of(144 * n, 144), 144)]
         return remote(block, block, ws.at[9 + n], wr.at[9 + n], other_core, p)
 
+    y_send(0, 0).start()
+    y_send(1, 0).start()
+
     zero8 = jnp.zeros((8, TOK), F32)
     ones8 = jnp.where(lax.broadcasted_iota(jnp.int32, (8, TOK), 0) == 0, 1.0, 0.0)
+    lower = x_lo == 0
+
+    def chunk_at(n):
+        if isinstance(n, int):
+            return lax.rem(z + (8 - (n + 1) // 2 if n % 2 else n // 2), 8)
+        return lax.rem(z + jnp.where(lax.rem(n, 2) == 1, 8 - (n + 1) // 2, n // 2), 8)
 
     def to_natural(slot):
         kt = qkv[slot, ROWS : 2 * ROWS, :].astype(F32)
         kt = jnp.concatenate([kt, jnp.zeros((128 - ROWS, TOK), F32)], axis=0)
-        kn[pl.ds(pl.multiple_of(slot * TOK, TOK), TOK), :] = kt.T.astype(BF16)
-
-    def pair_copy(at, n):
-        slot = qkv.at[x_lo * 8 + at]
-        return remote(stage.at[n], slot, xs.at[n], xr.at[n], f, x_pair)
-
-    def pair_in(at, n):
-        slot = qkv.at[(1 - x_lo) * 8 + at]
-        return remote(stage.at[n], slot, xs.at[n], xr.at[n], f, x_pair)
-
-    def project(at, n):
-        r = jnp.dot(nz[at], wc[...], preferred_element_type=F32)
+        kn[slot * TOK : slot * TOK + TOK, :] = kt.T.astype(BF16)
+
+    def pair_copy(n):
+        return remote(stage.at[n], qkv.at[2 * n + 1], xs.at[n], xr.at[n], f, x_pair)
+
+    def project(n):
+        r = jnp.dot(nz[chunk_at(n)], wc[...], preferred_element_type=F32)
         t = r.T
-        own = [t[0:72] * Q_SCALE, zero8, t[144:216], zero8, t[288:360], ones8]
-        oth = [t[72:144] * Q_SCALE, zero8, t[216:288], zero8, t[360:432], ones8]
+        own, oth = [], []
+        for part in range(3):
+            one = t[144 * part : 144 * part + 72]
+            two = t[144 * part + 72 : 144 * part + 144]
+            if part == 0:
+                one, two = one * Q_SCALE, two * Q_SCALE
+            own += [jnp.where(lower, one, two), ones8 if part == 2 else zero8]
+            oth += [jnp.where(lower, two, one), ones8 if part == 2 else zero8]
         stage[n] = jnp.concatenate(oth, axis=0).astype(BF16)
-        pair_copy(at, n).start()
-        qkv[x_lo * 8 + at] = jnp.concatenate(own, axis=0).astype(BF16)
-        to_natural(x_lo * 8 + at)
+        pair_copy(n).start()
+        qkv[2 * n] = jnp.concatenate(own, axis=0).astype(BF16)
+        to_natural(2 * n)
+
+    def receive(n):
+        pair_copy(n).wait()
+        to_natural(2 * n + 1)
 
     def z_forward(step):
         for sub in range(2):
@@ -185,6 +204,80 @@
                     if step < 3 and sends(step + 1, way, sub):
                         z_copy(step + 1, way, sub).start()
 
+    head = 2 * z + x_lo
+    scores = (score_a, score_b)
+    tops = (top_a, top_b)
+
+    def dest_of(slot, odd):
+        lo = 1 - x_lo if odd else x_lo
+        return lo * 8 + chunk_at(slot // 2)
+
+    def out_copy(slot, odd):
+        dest = dest_of(slot, odd)
+        return remote(ostage.at[slot], attn.at[head], os.at[slot], orr.at[head], f, dest)
+
+    def score_steps(slot, buf, keys):
+        q_t = qkv[slot, 0:ROWS, :]
+        state = [None]
+
+        def one(k):
+            s = jnp.dot(kn[k * TOK : k * TOK + TOK, 0:ROWS], q_t, preferred_element_type=F32)
+            scores[buf][k * TOK : k * TOK + TOK, :] = s
+            m = jnp.max(s.reshape(TOK // 8, 8, TOK), axis=0)
+            state[0] = m if state[0] is None else jnp.maximum(state[0], m)
+            if k == keys[-1]:
+                tops[buf][...] = state[0]
+
+        return [lambda k=k: one(k) for k in keys]
+
+    def job(slot, odd, buf, keys, first, last, next_slot):
+        steps = [] if next_slot is None else score_steps(next_slot, 1 - buf, keys)
+        m = jnp.max(tops[buf][...], axis=0, keepdims=True)
+        acc = None
+        if not first:
+            old = top_all[slot]
+            m = jnp.maximum(old, m)
+            acc = acc_all[slot] * jnp.exp2(old - m)
+        for n, k in enumerate(keys):
+            if steps:
+                steps[n]()
+            prob = jnp.exp2(scores[buf][k * TOK : k * TOK + TOK, :] - m).astype(BF16)
+            part = jnp.dot(qkv[k, 2 * ROWS : 3 * ROWS, :], prob, preferred_element_type=F32)
+            acc = part if acc is None else acc + part
+        if not last:
+            top_all[slot] = m
+            acc_all[slot] = acc
+            return
+        out = acc[0:HEAD] / acc[HEAD : HEAD + 1]
+        ostage[slot] = jnp.concatenate([out, zero8], axis=0).astype(BF16)
+        if odd:
+            out_copy(slot, odd).start()
+        else:
+            @pl.when(slot > 0)
+            def _():
+                out_copy(slot, odd).start()
+
+            @pl.when(slot == 0)
+            def _():
+                attn[head] = ostage[slot]
+
+    def attend(q0, q1, k0, k1, first, last):
+        keys = list(range(k0, k1))
+        for step in score_steps(q1 - 2, 0, keys):
+            step()
+        if q1 - q0 == 2:
+            job(q0, False, 0, keys, first, last, q0 + 1)
+            job(q0 + 1, True, 1, keys, first, last, None)
+            return
+
+        def two(i, c):
+            slot = q1 - 2 - 2 * i
+            job(slot, False, 0, keys, first, last, slot + 1)
+            job(slot + 1, True, 1, keys, first, last, jnp.maximum(slot - 2, q0))
+            return c
+
+        lax.fori_loop(0, (q1 - q0) // 2, two, 0)
+
     z_forward(0)
 
     def take_sel(i, c):
@@ -199,105 +292,76 @@
         b = wsel_all[2 * j + 1, 0:72, :].astype(F32)
         wc[144 * j : 144 * j + 144, :] = jnp.concatenate([a, b], axis=0).astype(BF16)
 
-    project(z, 0)
-    project(lax.rem(z + 7, 8), 1)
-    project(lax.rem(z + 1, 8), 2)
+    project(0)
+    project(1)
+    project(2)
+    receive(0)
+    attend(0, 2, 0, 2, True, False)
     z_forward(1)
     keep.wait()
+    core_send(y, 0).start()
     across_in.wait()
-    for sub in range(2):
-        for way in range(2):
-            y_send(way, sub).start()
-    core_send(2 * y).start()
-    core_send(2 * y + 1).start()
-    project(lax.rem(z + 6, 8), 3)
-    project(lax.rem(z + 2, 8), 4)
+    y_send(0, 1).start()
+    y_send(1, 1).start()
+    core_send(y, 1).start()
+    project(3)
+    project(4)
+    y_in(0, 0).wait_recv()
+    y_pass(0).start()
+    core_send(y_prev, 0).start()
+    y_in(1, 0).wait_recv()
+    core_send(y_next, 0).start()
+    receive(1)
+    receive(2)
+    attend(0, 2, 2, 6, False, False)
+    attend(2, 6, 0, 6, True, False)
     z_forward(2)
-    project(lax.rem(z + 5, 8), 5)
-    project(lax.rem(z + 3, 8), 6)
+    project(5)
+    project(6)
+    receive(3)
+    receive(4)
+    attend(0, 6, 6, 10, False, False)
+    attend(6, 10, 0, 10, True, False)
     z_forward(3)
-    project(lax.rem(z + 4, 8), 7)
+    project(7)
+    y_in(1, 1).wait_recv()
+    y_pass(1).start()
+    core_send(y_next, 1).start()
+    y_in(0, 1).wait_recv()
+    core_send(y_prev, 1).start()
+    receive(5)
+    receive(6)
+    attend(0, 10, 10, 14, False, False)
+    attend(10, 14, 0, 14, True, False)
+    receive(7)
+    attend(14, 16, 0, 16, True, True)
+    attend(0, 14, 14, 16, False, True)
+
+    y_pass_in(0).wait_recv()
+    core_send(y_far, 0).start()
+    y_pass_in(1).wait_recv()
+    core_send(y_far, 1).start()
     for step in range(4):
         for way in range(2):
             for sub in range(2):
                 if sends(step, way, sub):
                     z_copy(step, way, sub).wait_send()
-    order = [0, 7, 1, 6, 2, 5, 3, 4]
-    for n in range(8):
-        at = lax.rem(z + order[n], 8)
-        pair_copy(at, n).wait_send()
-        pair_in(at, n).wait_recv()
-        to_natural((1 - x_lo) * 8 + at)
-
-    head = 2 * z + x_lo
-    KB = 512
-
-    def attend(i, c):
-        dest = lax.rem(p + 1 + i, 16)
-        q_t = qkv[dest, 0:ROWS, :]
-        top = None
-        for kb in range(4096 // KB):
-            s = jnp.dot(
-                kn[kb * KB : (kb + 1) * KB, 0:ROWS], q_t, preferred_element_type=F32
-            )
-            new = jnp.max(s, axis=0, keepdims=True)
-            if top is not None:
-                new = jnp.maximum(top, new)
-            prob = jnp.exp2(s - new).astype(BF16)
-            part = None
-            for u in range(KB // TOK):
-                v_t = qkv[kb * (KB // TOK) + u, 2 * ROWS : 3 * ROWS, :]
-                o = jnp.dot(v_t, prob[u * TOK : (u + 1) * TOK], preferred_element_type=F32)
-                part = o if part is None else part + o
-            acc = part if top is None else acc * jnp.exp2(top - new) + part
-            top = new
-        out = acc[0:HEAD] / acc[HEAD : HEAD + 1]
-        ostage[i] = jnp.concatenate([out, zero8], axis=0).astype(BF16)
-
-        @pl.when(i < 15)
-        def _():
-            remote(ostage.at[i], attn.at[head], os.at[i], orr.at[head], f, dest).start()
-
-        @pl.when(i == 15)
-        def _():
-            attn[head] = ostage[i]
-
-        return c
-
-    lax.fori_loop(0, 5, attend, 0)
-    y_in(0, 0).wait_recv()
-    y_pass(0).start()
-    core_send(2 * y_prev).start()
-    y_in(1, 0).wait_recv()
-    core_send(2 * y_next).start()
-    lax.fori_loop(5, 11, attend, 0)
-    y_in(1, 1).wait_recv()
-    y_pass(1).start()
-    core_send(2 * y_next + 1).start()
-    y_in(0, 1).wait_recv()
-    core_send(2 * y_prev + 1).start()
-    lax.fori_loop(11, 16, attend, 0)
-
-    y_pass_in(0).wait_recv()
-    core_send(2 * y_far).start()
-    y_pass_in(1).wait_recv()
-    core_send(2 * y_far + 1).start()
-
-    def finish(i, c):
-        dest = lax.rem(p + 1 + i, 16)
-        src_head = 2 * lax.rem(dest, 8) + dest // 8
-        remote(ostage.at[i], attn.at[head], os.at[i], orr.at[head], f, dest).wait_send()
-        remote(ostage.at[i], attn.at[src_head], os.at[i], orr.at[src_head], f, dest).wait_recv()
-        return c
-
-    lax.fori_loop(0, 15, finish, 0)
+
+    for slot in range(1, 16):
+        src = dest_of(slot, slot % 2 == 1)
+        src_head = 2 * lax.rem(src, 8) + src // 8
+        out_copy(slot, slot % 2 == 1).wait_send()
+        remote(
+            ostage.at[slot], attn.at[src_head], os.at[slot], orr.at[src_head], f, src
+        ).wait_recv()
     for way in range(2):
-        for sub in range(2):
-            y_send(way, sub).wait_send()
+        for kind in range(2):
+            y_send(way, kind).wait_send()
         y_pass(way).wait_send()
-    for n in range(8):
-        core_send(n).wait_send()
-        core_in(n).wait_recv()
+    for at_y in (y, y_prev, y_next, y_far):
+        for kind in range(2):
+            core_send(at_y, kind).wait_send()
+            core_in(chip_of(at_y, kind)).wait_recv()
 
 
 def temporal_kernel(
@@ -419,6 +483,12 @@
             pltpu.VMEM((16, ROWS, TOK), BF16),
             pltpu.VMEM((ROWS, HALF), BF16),
             pltpu.VMEM((144, HALF), BF16),
+            pltpu.VMEM((4096, TOK), F32),
+            pltpu.VMEM((4096, TOK), F32),
+            pltpu.VMEM((8, TOK), F32),
+            pltpu.VMEM((8, TOK), F32),
+            pltpu.VMEM((16, 1, TOK), F32),
+            pltpu.VMEM((16, ROWS, TOK), F32),
             dma((16,)), dma((16,)),
             dma((16,)), dma((16,)),
             dma((8,)), dma((8,)),
@@ -461,13 +531,13 @@
 
 def body(hidden_states, modulation, w_qkv_spatial, w_out_spatial, w_qkv_temporal, w_out_temporal):
     p = lax.axis_index("patch")
-    x_lo, z = p // 8, lax.rem(p, 8)
+    z = lax.rem(p, 8)
     hid = hidden_states.reshape(TOK, D)
-    heads = w_qkv_spatial.reshape(HEAD, 3, HEADS, HEAD)
-    own = lax.dynamic_slice_in_dim(heads, 2 * z + x_lo, 1, axis=2)
-    other = lax.dynamic_slice_in_dim(heads, 2 * z + 1 - x_lo, 1, axis=2)
-    wsel = jnp.concatenate([own, other], axis=2).reshape(HEAD, 6 * HEAD)
-    wsel = jnp.pad(wsel, ((0, ROWS - HEAD), (0, 512 - 6 * HEAD)))
+    parts = [
+        lax.dynamic_slice_in_dim(w_qkv_spatial, D * part + 2 * HEAD * z, 2 * HEAD, axis=1)
+        for part in range(3)
+    ]
+    wsel = jnp.pad(jnp.concatenate(parts, axis=1), ((0, ROWS - HEAD), (0, 512 - 6 * HEAD)))
     rest = jnp.concatenate([w_out_spatial, w_qkv_temporal, w_out_temporal], axis=1)
     rest = jnp.pad(rest, ((0, ROWS - HEAD), (0, 2 * HALF - 5 * D)))
     rest = jnp.stack([rest[:, :HALF], rest[:, HALF:]])

time: 164 us -> 134 us (0.82)
  Pallas kernels: 157 us -> 128 us
  local copies, waits for them, and re-layouts: 5.78 us -> 2.96 us
    pallas_call x1, Pallas kernels: 126 us -> 96.5 us  [spatial_call(): pl.pallas_call(spatial_kernel, out_shape=(jax.ShapeDtypeStruct((HEADS, RO...]
    reshape x2 -> x0, local copies, waits for them, and re-layouts: 2.89 us -> none  [the longest x1 2.76 us: body(): heads = w_qkv_spatial.reshape(HEAD, 3, HEADS, HEAD)]
where the time goes in v2:
time: 134 us
  Pallas kernels  128 us (96%)
  other arithmetic  2.99 us (2%)
  local copies, waits for them, and re-layouts  2.96 us (2%)
    pallas_call x1, Pallas kernels, spatial_call(): pl.pallas_call(spatial_kernel, out_shape=(jax.ShapeDtypeStruct((HEADS, RO...  96.5 us
    pallas_call x1, Pallas kernels, temporal_call(): pl.pallas_call(temporal_kernel, out_shape=jax.ShapeDtypeStruct((TOK, D),...  31.3 us

profile of v2, /device:TPU:1, one launch (start us, length us, event | category | flops | bytes accessed | tf_op | source)
XLA Modules:
  0.0 133.7 jit_solution(7734952586499584615)
XLA Ops:
  0.0 1.0 constant_dynamic-slice_fusion.2
  1.0 0.7 fusion.17.wsel
  1.7 1.2 fusion.8
  2.9 0.1 slice_bitcast_fusion.1
  3.0 1.0 pad_maximum_fusion.wrest
  4.0 96.5 %spatial.1 = (bf16[16,80,256]{2,1,0:T(8,128)(2,1)}, bf16[2,1152,2944]{2,1,0:T(8,128)(2,1)}) custom-call(bf16[256,1152]{1,0:T(8,128)(2,1)} %bitcast.6, f32[6,1152]{1,0:T(8,128)} %mod.3, bf16[80,512]{1,0:T(8,128)(2,1)} %fusion.17.wsel, bf16[2,80,2944]{2,1,0:T(8,128)(2,1)} %pad_maximum_fusion.wrest), custom_call_target="tpu_custom_call" | custom-call | tf_op jit(solution)/shard_map/spatial/pallas_call | solution.py:468
  100.5 31.3 %temporal.1 = bf16[256,1152]{1,0:T(8,128)(2,1)} custom-call(bf16[256,1152]{1,0:T(8,128)(2,1)} %bitcast.7, f32[6,1152]{1,0:T(8,128)} %mod.3, bf16[16,80,256]{2,1,0:T(8,128)(2,1)} %get-tuple-element.7.attn, bf16[2,1152,2944]{2,1,0:T(8,128)(2,1)} %get-tuple-element.8.wfull), custom_call_target="tpu_custom_call" | custom-call | tf_op jit(solution)/shard_map/temporal/pallas_call | solution.py:507
  131.8 1.9 %copy.8 = bf16[1,256,1152]{2,1,0:T(8,128)(2,1)} copy(bf16[1,256,1152]{2,1,0:T(8,128)(2,1)} %bitcast.8) | data formatting | bytes 1179648

commit v3 on v2

v3 whole, which is shorter than its diff:
```python
import math

import jax
import jax.numpy as jnp
from jax import lax
from jax.experimental import pallas as pl
from jax.experimental.pallas import tpu as pltpu
from jax.sharding import PartitionSpec as P

HEAD = 72
HEADS = 16
D = 1152
TOK = 256
ROWS = 80
HALF = 2944
Q_SCALE = HEAD ** (-0.5) * math.log2(math.e)
F32 = jnp.float32
BF16 = jnp.bfloat16


def remote(src, dst, send, recv, frame, patch):
    return pltpu.make_async_remote_copy(
        src_ref=src,
        dst_ref=dst,
        send_sem=send,
        recv_sem=recv,
        device_id={"frame": frame, "patch": patch},
        device_id_type=pl.DeviceIdType.MESH,
    )


def signal(sem, frame, patch):
    pl.semaphore_signal(
        sem, inc=1, device_id={"frame": frame, "patch": patch}, device_id_type=pl.DeviceIdType.MESH
    )


def norm_modulate(x, shift, scale):
    centred = x - jnp.mean(x, axis=-1, keepdims=True)
    variance = jnp.mean(centred * centred, axis=-1, keepdims=True)
    return centred * lax.rsqrt(variance + 1e-06) * (1.0 + scale) + shift


def block_kernel(
    hid, mod, wsel, wrest, out,
    nz, wsel_all, wc, qkv, stage, kn, ostage, attn, w1, w, score_a, score_b, top_a, top_b, top_all, acc_all,
    at32, mid, midt, proj, qkv_t, acc_t, osend,
    zs, zr, ss, sr, xs, xr, os, orr, ws, wr, ms, mr, bs, br,
):
    f = lax.axis_index("frame")
    p = lax.axis_index("patch")
    core = lax.rem(f, 2)
    x_hi = lax.rem(f // 2, 2)
    y = f // 4
    x_lo = p // 8
    z = lax.rem(p, 8)
    chip = f // 2
    other_core = f + 1 - 2 * core
    cross_f = (y * 2 + 1 - x_hi) * 2 + core
    x_pair = (1 - x_lo) * 8 + z
    y_up = lax.rem(y + 1, 4) * 4 + x_hi * 2 + core
    y_dn = lax.rem(y + 3, 4) * 4 + x_hi * 2 + core
    z_up = x_lo * 8 + lax.rem(z + 1, 8)
    z_dn = x_lo * 8 + lax.rem(z + 7, 8)

    barrier = pltpu.get_barrier_semaphore()

    def greet(i, c):
        signal(barrier, lax.rem(f + i, 16), p)
        signal(barrier, f, lax.rem(p + i, 16))
        return c

    lax.fori_loop(1, 16, greet, 0)
    signal(barrier, cross_f, x_pair)
    nz[0] = norm_modulate(hid[...].astype(F32), mod[0:1], mod[1:2]).astype(BF16)
    pl.semaphore_wait(barrier, 31)

    def z_block(g, way):
        return nz.at[g, pl.ds(128 * way, 128)]

    def z_hop(g, way):
        if g <= 2:
            source = nz.at[0, pl.ds(128 * (g - 1), 128)]
        elif g <= 6:
            source = z_block(g - 2, way)
        else:
            source = z_block(5 + way, way)
        n = 2 * g + way
        return remote(source, z_block(g, way), zs.at[n], zr.at[n], f, z_dn if way else z_up)

    for g in (1, 2):
        for way in range(2):
            z_hop(g, way).start()

    def arrive(g):
        for way in range(2):
            z_hop(g, way).wait_recv()
            if g <= 4:
                z_hop(g + 2, way).start()
            elif g == 5 + way:
                z_hop(7, way).start()

    first = remote(wrest.at[1 - core], w1, ws.at[0], wr.at[0], other_core, p)
    first.start()

    def sel_copy(source, peer, n):
        return remote(source, wsel_all.at[n], ss.at[n], sr.at[n], peer, p)

    sel_copy(wsel, other_core, f).start()

    def sel_send(i, c):
        peer = lax.rem(f + 2 * i, 16)
        remote(wsel, wsel_all.at[f], ss.at[peer], sr.at[f], peer, p).start()
        return c

    lax.fori_loop(1, 8, sel_send, 0)
    wsel_all[f] = wsel[...]

    first.wait()
    mine = wrest[core, 0:72, :].astype(F32)
    theirs = w1[0:72, :].astype(F32)
    is_first = core == 0
    low = jnp.where(is_first, mine, theirs)
    high = jnp.where(is_first, theirs, mine)
    w[core, pl.ds(pl.multiple_of(144 * chip, 144), 144), :] = jnp.concatenate(
        [low, high], axis=0
    ).astype(BF16)

    def chip_of(at_y, kind):
        return 2 * at_y + (x_hi if kind == 0 else 1 - x_hi)

    def rows(half, n, start, size):
        return w.at[half, pl.ds(pl.multiple_of(144 * n + start, 16), size)]

    y_prev = lax.rem(y + 3, 4)
    y_next = lax.rem(y + 1, 4)
    y_far = lax.rem(y + 2, 4)

    def cross_send(far):
        block = rows(core, chip_of(y_far if far else y, 0), 0, 144)
        return remote(block, block, ws.at[1 + far], wr.at[1 + far], cross_f, x_pair)

    def y_send(way, kind):
        n = 3 + way * 2 + kind
        block = rows(core, chip_of(y, kind), 0, 144)
        return remote(block, block, ws.at[n], wr.at[n], y_dn if way else y_up, p)

    def y_pass(way):
        block = rows(core, chip_of(y_next if way else y_prev, 0), 80 * way, 64 if way else 80)
        return remote(block, block, ws.at[7 + way], wr.at[7 + way], y_dn if way else y_up, p)

    def core_send(at_y, kind):
        n = chip_of(at_y, kind)
        block = rows(core, n, 0, 144)
        return remote(block, block, ws.at[9 + n], wr.at[9 + n], other_core, p)

    cross_send(0).start()
    for way in range(2):
        y_send(way, 0).start()
    core_send(y, 0).start()

    zero8 = jnp.zeros((8, TOK), F32)
    ones8 = jnp.where(lax.broadcasted_iota(jnp.int32, (8, TOK), 0) == 0, 1.0, 0.0)
    lower = x_lo == 0

    def to_natural(slot):
        kt = qkv[slot, ROWS : 2 * ROWS, :].astype(F32)
        kt = jnp.concatenate([kt, jnp.zeros((128 - ROWS, TOK), F32)], axis=0)
        kn[slot * TOK : slot * TOK + TOK, :] = kt.T.astype(BF16)

    def pair_copy(g):
        return remote(stage.at[g], qkv.at[2 * g + 1], xs.at[g], xr.at[g], f, x_pair)

    def project(g):
        r = jnp.dot(nz[g], wc[...], preferred_element_type=F32)
        t = r.T
        own, oth = [], []
        for part in range(3):
            one = t[144 * part : 144 * part + 72]
            two = t[144 * part + 72 : 144 * part + 144]
            if part == 0:
                one, two = one * Q_SCALE, two * Q_SCALE
            own += [jnp.where(lower, one, two), ones8 if part == 2 else zero8]
            oth += [jnp.where(lower, two, one), ones8 if part == 2 else zero8]
        stage[g] = jnp.concatenate(oth, axis=0).astype(BF16)
        pair_copy(g).start()
        qkv[2 * g] = jnp.concatenate(own, axis=0).astype(BF16)
        to_natural(2 * g)

    def receive(g):
        pair_copy(g).wait()
        to_natural(2 * g + 1)

    head = 2 * z + x_lo
    scores = (score_a, score_b)
    tops = (top_a, top_b)
    top_all[...] = jnp.full(top_all.shape, -1e30, F32)
    acc_all[...] = jnp.zeros(acc_all.shape, F32)

    def out_copy(g, odd, half):
        s = (g + 1) // 2
        if isinstance(g, int):
            j = half if g in (0, 7) else (g + 1) % 2
        else:
            j = lax.rem(g + 1, 2)
        to = (1 - x_lo if odd else x_lo) * 8 + lax.rem(z + (s if half else 8 - s), 8)
        n = 2 * odd + half
        return remote(
            ostage.at[g, n], attn.at[head, j], os.at[4 * g + n], orr.at[2 * head + j], f, to
        )

    def score_steps(gq, gk, buf):
        q_t = jnp.concatenate([qkv[2 * gq, 0:ROWS, :], qkv[2 * gq + 1, 0:ROWS, :]], axis=1)
        state = [None]

        def one(u):
            at = pl.ds(pl.multiple_of(2 * TOK * gk + TOK * u, TOK), TOK)
            s = jnp.dot(kn[at, 0:ROWS], q_t, preferred_element_type=F32)
            scores[buf][TOK * u : TOK * u + TOK, :] = s
            m = jnp.max(s.reshape(TOK // 8, 8, 2 * TOK), axis=0)
            state[0] = m if state[0] is None else jnp.maximum(state[0], m)
            if u == 1:
                tops[buf][...] = state[0]

        return [lambda: one(0), lambda: one(1)]

    def job(gq, gk, buf, following, last):
        steps = score_steps(*following, 1 - buf) if following else None
        old = top_all[gq]
        m = jnp.maximum(old, jnp.max(tops[buf][...], axis=0, keepdims=True))
        acc = acc_all[gq] * jnp.exp2(old - m)
        for u in range(2):
            if steps:
                steps[u]()
            prob = jnp.exp2(scores[buf][TOK * u : TOK * u + TOK, :] - m).astype(BF16)
            acc += jnp.dot(
                qkv[2 * gk + u, 2 * ROWS : 3 * ROWS, :], prob, preferred_element_type=F32
            )
        if not last:
            top_all[gq] = m
            acc_all[gq] = acc
            return
        o = acc[0:HEAD] / acc[HEAD : HEAD + 1]
        o = jnp.concatenate([o, jnp.zeros((8, 2 * TOK), F32)], axis=0).astype(BF16)
        for odd in range(2):
            for half in range(2):
                n = 2 * odd + half
                ostage[gq, n] = o[:, 128 * n : 128 * n + 128]
                if isinstance(gq, int) and gq == 0 and odd == 0:
                    attn[head, half] = ostage[gq, n]
                else:
                    out_copy(gq, odd, half).start()

    def jobs(pick, count, last):
        for step in score_steps(*pick(0), 0):
            step()
        rest = 1 if count % 2 else 2

        def two(i, c):
            job(*pick(2 * i), 0, pick(2 * i + 1), last == "all")
            job(*pick(2 * i + 1), 1, pick(2 * i + 2), last == "all")
            return c

        if count > rest:
            lax.fori_loop(0, (count - rest) // 2, two, 0)
        for t in range(count - rest, count):
            following = pick(t + 1) if t + 1 < count else None
            end = last == "all" or (last == "end" and t == count - 1)
            job(*pick(t), (t - count + rest) % 2, following, end)

    def group_jobs(g):
        def pick(t):
            if isinstance(t, int):
                return (t, g) if t < g else (g, t - g)
            return jnp.where(t < g, t, g), jnp.where(t < g, g, t - g)

        jobs(pick, 2 * g + 1, "")

    arrive(1)

    def sel_take(i, c):
        peer = lax.rem(f + 2 * i, 16)
        sel_copy(wsel, peer, peer).wait_recv()
        remote(
            wsel_all.at[peer], wsel_all.at[peer], ss.at[peer + 1 - 2 * core], sr.at[peer], other_core, p
        ).start()
        return c

    lax.fori_loop(1, 8, sel_take, 0)

    def sel_swapped(i, c):
        n = lax.rem(other_core + 2 * i, 16)
        sel_copy(wsel, other_core, n).wait_recv()
        return c

    lax.fori_loop(0, 8, sel_swapped, 0)
    for j in range(8):
        a = wsel_all[2 * j, 0:72, :].astype(F32)
        b = wsel_all[2 * j + 1, 0:72, :].astype(F32)
        wc[144 * j : 144 * j + 144, :] = jnp.concatenate([a, b], axis=0).astype(BF16)
    project(0)
    project(1)
    arrive(2)
    project(2)
    receive(0)
    receive(1)
    group_jobs(0)
    group_jobs(1)
    arrive(3)
    project(3)
    receive(2)
    group_jobs(2)
    arrive(4)
    cross_send(0).wait_recv()
    for way in range(2):
        y_send(way, 0).wait_recv()
        y_pass(way).start()
    for way in range(2):
        y_send(way, 1).start()
    core_send(y, 1).start()
    core_send(y_prev, 0).start()
    core_send(y_next, 0).start()
    project(4)
    receive(3)
    group_jobs(3)
    arrive(5)
    project(5)
    receive(4)
    group_jobs(4)
    arrive(6)
    far = [rows(core, chip_of(y_far, 0), 80 * way, 64 if way else 80) for way in range(2)]
    for way in range(2):
        remote(far[way], far[way], ws.at[7 + way], wr.at[7 + way], other_core, p).wait_recv()
    cross_send(1).start()
    core_send(y_far, 0).start()
    project(6)
    receive(5)
    group_jobs(5)
    arrive(7)
    project(7)
    receive(6)
    group_jobs(6)
    receive(7)
    jobs(lambda t: (6 - t, 7), 7, "all")
    jobs(lambda t: (7, t), 8, "end")

    for way in range(2):
        y_send(way, 1).wait_recv()
    core_send(y_prev, 1).start()
    core_send(y_next, 1).start()
    cross_send(1).wait_recv()
    core_send(y_far, 1).start()

    def out_take(i, c):
        src = lax.rem(p + i, 16)
        n = 2 * (2 * lax.rem(src, 8) + src // 8)
        for j in range(2):
            here = attn.at[n // 2, j]
            remote(ostage.at[0, 0], here, os.at[0], orr.at[n + j], f, src).wait_recv()
        return c

    lax.fori_loop(1, 16, out_take, 0)
    for h in range(HEADS):
        at32[HEAD * h : HEAD * h + HEAD, :] = jnp.concatenate(
            [attn[h, 0, 0:HEAD, :], attn[h, 1, 0:HEAD, :]], axis=1
        ).astype(F32)
    for j in range(9):
        proj[:, 128 * j : 128 * j + 128] = at32[128 * j : 128 * j + 128, :].T.astype(BF16)

    for at_y in (y, y_prev, y_next, y_far):
        for kind in range(2):
            n = chip_of(at_y, kind)
            block = rows(1 - core, n, 0, 144)
            remote(block, block, ws.at[9 + n], wr.at[9 + n], other_core, p).wait_recv()

    r = jnp.dot(proj[...], w[0, :, 0:D], preferred_element_type=F32)
    mid[...] = (hid[...].astype(F32) + mod[2:3] * r).astype(BF16)

    def rows16(ref, n):
        return ref.at[pl.ds(pl.multiple_of(16 * n, 16), 16)]

    def send_mid(i, c):
        peer = lax.rem(f + i, 16)
        remote(rows16(mid, peer), rows16(midt, f), ms.at[i], mr.at[f], peer, p).start()
        return c

    lax.fori_loop(1, 16, send_mid, 0)
    here = pl.ds(pl.multiple_of(16 * f, 16), 16)
    midt[here, :] = mid[here, :]

    for g in range(1, 8):
        for way in range(2):
            z_hop(g, way).wait_send()

    def sel_sent(i, c):
        sel_copy(wsel, other_core, lax.rem(f + 2 * i, 16)).wait_send()
        sel_copy(wsel, other_core, lax.rem(other_core + 2 * i, 16)).wait_send()
        return c

    lax.fori_loop(1, 8, sel_sent, 0)
    sel_copy(wsel, other_core, f).wait_send()

    def out_sent(n, c):
        remote(ostage.at[0, 0], attn.at[0, 0], os.at[n], orr.at[0], f, x_pair).wait_send()
        return c

    lax.fori_loop(2, 32, out_sent, 0)
    for way in range(2):
        cross_send(way).wait_send()
        y_pass(way).wait_send()
        for kind in range(2):
            y_send(way, kind).wait_send()
    for at_y in (y, y_prev, y_next, y_far):
        for kind in range(2):
            core_send(at_y, kind).wait_send()

    def take_mid(i, c):
        peer = lax.rem(f + i, 16)
        remote(rows16(mid, peer), rows16(midt, peer), ms.at[i], mr.at[peer], peer, p).wait()
        return c

    lax.fori_loop(1, 16, take_mid, 0)
    proj[...] = norm_modulate(midt[...].astype(F32), mod[3:4], mod[4:5]).astype(BF16)
    a = jnp.dot(proj[...], w[0, :, D:HALF], preferred_element_type=F32)
    qkv_t[:, 0:D] = (a[:, 0:D] * Q_SCALE).astype(BF16)
    qkv_t[:, D : HALF - D] = a[:, D:].astype(BF16)
    b = jnp.dot(proj[...], w[1, :, 0 : 4 * D - HALF], preferred_element_type=F32)
    qkv_t[:, HALF - D : 3 * D] = b.astype(BF16)

    ri = lax.broadcasted_iota(jnp.int32, (TOK, TOK), 0)
    ci = lax.broadcasted_iota(jnp.int32, (TOK, TOK), 1)
    same = lax.rem(ri, 16) == lax.rem(ci, 16)
    acc_t[...] = jnp.zeros_like(acc_t)
    for h in range(HEADS):
        start = 128 * min(HEAD * h // 128, 7)
        low = HEAD * h - start
        inside = (ci >= low) & (ci < low + HEAD)
        q = qkv_t[:, start : start + 256]
        q = jnp.where(inside, q, jnp.zeros_like(q))
        k = qkv_t[:, D + start : D + start + 256]
        v = qkv_t[:, 2 * D + start : 2 * D + start + 256]
        s = lax.dot_general(q, k, (((1,), (1,)), ((), ())), preferred_element_type=F32)
        s = jnp.where(same, s, -1e30)
        prob = jnp.exp2(s - jnp.max(s, axis=1, keepdims=True))
        total = jnp.sum(prob, axis=1, keepdims=True)
        o = jnp.dot(prob.astype(BF16), v, preferred_element_type=F32) / total
        acc_t[:, start : start + 256] = jnp.where(inside, o, acc_t[:, start : start + 256])
    r = jnp.dot(
        acc_t[...].astype(BF16), w[1, :, 4 * D - HALF : 5 * D - HALF], preferred_element_type=F32
    )
    osend[...] = (midt[...].astype(F32) + mod[5:6] * r).astype(BF16)

    def send_out(i, c):
        peer = lax.rem(f + i, 16)
        remote(rows16(osend, peer), rows16(out, f), bs.at[i], br.at[f], peer, p).start()
        return c

    lax.fori_loop(1, 16, send_out, 0)
    out[here, :] = osend[here, :]

    def take_out(i, c):
        peer = lax.rem(f + i, 16)
        remote(rows16(osend, peer), rows16(out, peer), bs.at[i], br.at[peer], peer, p).wait()
        return c

    lax.fori_loop(1, 16, take_out, 0)


VMEM = pl.BlockSpec(memory_space=pltpu.VMEM)


def block_call(hid, mod, wsel, wrest):
    dma = pltpu.SemaphoreType.DMA
    return pl.pallas_call(
        block_kernel,
        out_shape=jax.ShapeDtypeStruct((TOK, D), BF16),
        in_specs=[VMEM] * 4,
        out_specs=VMEM,
        scratch_shapes=[
            pltpu.VMEM((8, TOK, D), BF16),
            pltpu.VMEM((16, ROWS, 512), BF16),
            pltpu.VMEM((D, 512), BF16),
            pltpu.VMEM((16, 3 * ROWS, TOK), BF16),
            pltpu.VMEM((8, 3 * ROWS, TOK), BF16),
            pltpu.VMEM((4096, 128), BF16),
            pltpu.VMEM((8, 4, ROWS, 128), BF16),
            pltpu.VMEM((HEADS, 2, ROWS, 128), BF16),
            pltpu.VMEM((ROWS, HALF), BF16),
            pltpu.VMEM((2, D, HALF), BF16),
            pltpu.VMEM((2 * TOK, 2 * TOK), F32),
            pltpu.VMEM((2 * TOK, 2 * TOK), F32),
            pltpu.VMEM((8, 2 * TOK), F32),
            pltpu.VMEM((8, 2 * TOK), F32),
            pltpu.VMEM((8, 1, 2 * TOK), F32),
            pltpu.VMEM((8, ROWS, 2 * TOK), F32),
            pltpu.VMEM((D, TOK), F32),
            pltpu.VMEM((TOK, D), BF16),
            pltpu.VMEM((TOK, D), BF16),
            pltpu.VMEM((TOK, D), BF16),
            pltpu.VMEM((TOK, 3 * D), BF16),
            pltpu.VMEM((TOK, D), F32),
            pltpu.VMEM((TOK, D), BF16),
            dma((16,)), dma((16,)),
            dma((16,)), dma((16,)),
            dma((8,)), dma((8,)),
            dma((32,)), dma((32,)),
            dma((17,)), dma((17,)),
            dma((16,)), dma((16,)),
            dma((16,)), dma((16,)),
        ],
        compiler_params=pltpu.CompilerParams(
            collective_id=0, has_side_effects=True, vmem_limit_bytes=60 * 1024 * 1024
        ),
        name="block",
    )(hid, mod, wsel, wrest)


def body(hidden_states, modulation, w_qkv_spatial, w_out_spatial, w_qkv_temporal, w_out_temporal):
    p = lax.axis_index("patch")
    z = lax.rem(p, 8)
    hid = hidden_states.reshape(TOK, D)
    parts = [
        lax.dynamic_slice_in_dim(w_qkv_spatial, D * part + 2 * HEAD * z, 2 * HEAD, axis=1)
        for part in range(3)
    ]
    wsel = jnp.pad(jnp.concatenate(parts, axis=1), ((0, ROWS - HEAD), (0, 512 - 6 * HEAD)))
    rest = jnp.concatenate([w_out_spatial, w_qkv_temporal, w_out_temporal], axis=1)
    rest = jnp.pad(rest, ((0, ROWS - HEAD), (0, 2 * HALF - 5 * D)))
    rest = jnp.stack([rest[:, :HALF], rest[:, HALF:]])
    out = block_call(hid, modulation, wsel, rest)
    return out.reshape(1, TOK, D)


def solution(mesh):
    in_specs = (
        P("frame", "patch", None),
        P(),
        P("frame", None),
        P("frame", None),
        P("frame", None),
        P("frame", None),
    )
    out_specs = P("frame", "patch", None)
    return jax.shard_map(body, mesh=mesh, in_specs=in_specs, out_specs=out_specs, check_vma=False)
```

time: 134 us -> 114 us (0.85)
  Pallas kernels: 128 us -> 108 us
    pallas_call x2 -> x1, Pallas kernels: 128 us -> 108 us  [block_call(): pl.pallas_call(block_kernel, out_shape=jax.ShapeDtypeStruct((TOK, D), BF1...]
where the time goes in v3:
time: 114 us
  Pallas kernels  108 us (95%)
  other arithmetic  2.99 us (3%)
  local copies, waits for them, and re-layouts  2.96 us (3%)
    pallas_call x1, Pallas kernels, block_call(): pl.pallas_call(block_kernel, out_shape=jax.ShapeDtypeStruct((TOK, D), BF1...  108 us

profile of v3, /device:TPU:1, one launch (start us, length us, event | category | flops | bytes accessed | tf_op | source)
XLA Modules:
  0.0 114.0 jit_solution(15188920413654609401)
XLA Ops:
  0.0 1.0 constant_dynamic-slice_fusion.2
  1.0 0.7 fusion.17.wsel
  1.7 1.2 %fusion.8 = bf16[80,5888]{1,0:T(8,128)(2,1)S(1)} fusion(bf16[72,1152]{1,0:T(8,128)(2,1)} %param.11, bf16[72,3456]{1,0:T(8,128)(2,1)} %param.10, bf16[72,1152]{1,0:T(8,128)(2,1)} %param.9), kind=kLoop, calls=%fused_computation.10 | loop fusion | flops 7065600 | bytes 1771520 | tf_op jit(solution)/shard_map/concatenate | solution.py:527
  2.9 0.1 slice_bitcast_fusion.1
  3.0 1.0 pad_maximum_fusion.wrest
  4.0 108.0 %block.1 = bf16[256,1152]{1,0:T(8,128)(2,1)} custom-call(bf16[256,1152]{1,0:T(8,128)(2,1)} %bitcast.7, f32[6,1152]{1,0:T(8,128)} %mod.1, bf16[80,512]{1,0:T(8,128)(2,1)} %fusion.17.wsel, bf16[2,80,2944]{2,1,0:T(8,128)(2,1)} %pad_maximum_fusion.wrest), custom_call_target="tpu_custom_call" | custom-call | tf_op jit(solution)/shard_map/block/pallas_call | solution.py:474
  112.1 1.9 %copy.8 = bf16[1,256,1152]{2,1,0:T(8,128)(2,1)} copy(bf16[1,256,1152]{2,1,0:T(8,128)(2,1)} %bitcast.6) | data formatting | bytes 1179648

commit v4 on v3

--- a/solution.py
+++ b/solution.py
@@ -42,9 +42,9 @@
 
 
 def block_kernel(
-    hid, mod, wsel, wrest, out,
-    nz, wsel_all, wc, qkv, stage, kn, ostage, attn, w1, w, score_a, score_b, top_a, top_b, top_all, acc_all,
-    at32, mid, midt, proj, qkv_t, acc_t, osend,
+    hid, mod, w_qkv_s, w_out_s, w_qkv_t, w_out_t, out,
+    nz, wsel, wrest, wo, wsel_all, wc, qkv, stage, kn, ostage, attn, w1, w, score_a, score_b, top_a, top_b, top_all, acc_all,
+    mid, midt, proj, qkv_t, acc_t, osend,
     zs, zr, ss, sr, xs, xr, os, orr, ws, wr, ms, mr, bs, br,
 ):
     f = lax.axis_index("frame")
@@ -73,6 +73,31 @@
     lax.fori_loop(1, 16, greet, 0)
     signal(barrier, cross_f, x_pair)
     nz[0] = norm_modulate(hid[...].astype(F32), mod[0:1], mod[1:2]).astype(BF16)
+
+    lanes = lax.broadcasted_iota(jnp.int32, (HEAD, TOK), 1)
+    parts = []
+    for part in range(3):
+        at = pl.ds(pl.multiple_of(D * part + 128 * z, 128), TOK)
+        window = w_qkv_s[:, at].astype(F32)
+        window = pltpu.roll(window, lax.rem(TOK - 16 * z + 16 * part, TOK), axis=1)
+        inside = (lanes >= 16 * part) & (lanes < 16 * part + 2 * HEAD)
+        parts.append(jnp.where(inside, window, 0.0))
+    q, k, v = parts
+    sel = jnp.concatenate(
+        [q[:, 0:128], q[:, 128:] + k[:, 0:128], k[:, 128:] + v[:, 0:128], v[:, 128:]], axis=1
+    )
+
+    def to_rows(value):
+        tail = jnp.zeros((ROWS - HEAD, value.shape[1]), F32)
+        return jnp.concatenate([value.astype(F32), tail], axis=0).astype(BF16)
+
+    wsel[...] = to_rows(sel)
+    cut = HALF - D
+    wrest[0, :, 0:D] = to_rows(w_out_s[...])
+    wrest[0, :, D:HALF] = to_rows(w_qkv_t[:, 0:cut])
+    wrest[1, :, 0 : 3 * D - cut] = to_rows(w_qkv_t[:, cut:])
+    wrest[1, :, 3 * D - cut : 4 * D - cut] = to_rows(w_out_t[...])
+    wrest[1, :, 4 * D - cut :] = jnp.zeros((ROWS, HALF - 4 * D + cut), BF16)
     pl.semaphore_wait(barrier, 31)
 
     def z_block(g, way):
@@ -197,17 +222,29 @@
     top_all[...] = jnp.full(top_all.shape, -1e30, F32)
     acc_all[...] = jnp.zeros(acc_all.shape, F32)
 
-    def out_copy(g, odd, half):
-        s = (g + 1) // 2
-        if isinstance(g, int):
-            j = half if g in (0, 7) else (g + 1) % 2
+    def out_copy(d, odd, half):
+        to = (1 - x_lo if odd else x_lo) * 8 + lax.rem(z + (d if half else 8 - d), 8)
+        n = 2 * odd + half
+        return remote(ostage.at[d, n], attn.at[head], os.at[4 * d + n], orr.at[head], f, to)
+
+    def emit(d, odd, half, first_rows, last_rows):
+        n = 2 * odd + half
+        ostage[d, n] = jnp.concatenate([first_rows, last_rows], axis=0).astype(BF16)
+        if isinstance(d, int) and d == 0 and odd == 0:
+            attn[head] = ostage[d, n]
         else:
-            j = lax.rem(g + 1, 2)
-        to = (1 - x_lo if odd else x_lo) * 8 + lax.rem(z + (s if half else 8 - s), 8)
-        n = 2 * odd + half
-        return remote(
-            ostage.at[g, n], attn.at[head, j], os.at[4 * g + n], orr.at[2 * head + j], f, to
-        )
+            out_copy(d, odd, half).start()
+
+    def emit_single(d, o):
+        for odd in range(2):
+            at = 256 * odd
+            emit(d, odd, 0, o[:, at : at + 128], o[:, at + 128 : at + 256])
+
+    def emit_pair(d, o0, o1):
+        for odd in range(2):
+            for half in range(2):
+                at = 128 * (2 * odd + half)
+                emit(d, odd, half, o0[:, at : at + 128], o1[:, at : at + 128])
 
     def score_steps(gq, gk, buf):
         q_t = jnp.concatenate([qkv[2 * gq, 0:ROWS, :], qkv[2 * gq + 1, 0:ROWS, :]], axis=1)
@@ -236,45 +273,40 @@
             acc += jnp.dot(
                 qkv[2 * gk + u, 2 * ROWS : 3 * ROWS, :], prob, preferred_element_type=F32
             )
-        if not last:
-            top_all[gq] = m
-            acc_all[gq] = acc
-            return
-        o = acc[0:HEAD] / acc[HEAD : HEAD + 1]
-        o = jnp.concatenate([o, jnp.zeros((8, 2 * TOK), F32)], axis=0).astype(BF16)
-        for odd in range(2):
-            for half in range(2):
-                n = 2 * odd + half
-                ostage[gq, n] = o[:, 128 * n : 128 * n + 128]
-                if isinstance(gq, int) and gq == 0 and odd == 0:
-                    attn[head, half] = ostage[gq, n]
-                else:
-                    out_copy(gq, odd, half).start()
-
-    def jobs(pick, count, last):
+        if last:
+            return acc[0:HEAD] / acc[HEAD : HEAD + 1]
+        top_all[gq] = m
+        acc_all[gq] = acc
+
+    def jobs(pick, count, finish=None):
+        last = finish is not None
         for step in score_steps(*pick(0), 0):
             step()
         rest = 1 if count % 2 else 2
 
         def two(i, c):
-            job(*pick(2 * i), 0, pick(2 * i + 1), last == "all")
-            job(*pick(2 * i + 1), 1, pick(2 * i + 2), last == "all")
+            o1 = job(*pick(2 * i), 0, pick(2 * i + 1), last)
+            o0 = job(*pick(2 * i + 1), 1, pick(2 * i + 2), last)
+            if last:
+                finish(i, o0, o1)
             return c
 
         if count > rest:
             lax.fori_loop(0, (count - rest) // 2, two, 0)
         for t in range(count - rest, count):
             following = pick(t + 1) if t + 1 < count else None
-            end = last == "all" or (last == "end" and t == count - 1)
-            job(*pick(t), (t - count + rest) % 2, following, end)
-
-    def group_jobs(g):
+            o = job(*pick(t), (t - count + rest) % 2, following, last)
+        if last:
+            finish(None, o, None)
+
+    def group_jobs(g, begin, end):
         def pick(t):
+            t = t + begin
             if isinstance(t, int):
                 return (t, g) if t < g else (g, t - g)
             return jnp.where(t < g, t, g), jnp.where(t < g, g, t - g)
 
-        jobs(pick, 2 * g + 1, "")
+        jobs(pick, end - begin)
 
     arrive(1)
 
@@ -304,12 +336,12 @@
     project(2)
     receive(0)
     receive(1)
-    group_jobs(0)
-    group_jobs(1)
+    group_jobs(0, 0, 1)
+    group_jobs(1, 0, 3)
     arrive(3)
     project(3)
     receive(2)
-    group_jobs(2)
+    group_jobs(2, 0, 5)
     arrive(4)
     cross_send(0).wait_recv()
     for way in range(2):
@@ -322,27 +354,37 @@
     core_send(y_next, 0).start()
     project(4)
     receive(3)
-    group_jobs(3)
+    group_jobs(3, 0, 7)
     arrive(5)
     project(5)
     receive(4)
-    group_jobs(4)
+    group_jobs(4, 0, 9)
+    receive(5)
+    group_jobs(5, 0, 4)
     arrive(6)
+    project(6)
+    group_jobs(5, 4, 11)
     far = [rows(core, chip_of(y_far, 0), 80 * way, 64 if way else 80) for way in range(2)]
     for way in range(2):
         remote(far[way], far[way], ws.at[7 + way], wr.at[7 + way], other_core, p).wait_recv()
     cross_send(1).start()
     core_send(y_far, 0).start()
-    project(6)
-    receive(5)
-    group_jobs(5)
+    receive(6)
+    group_jobs(6, 0, 4)
     arrive(7)
     project(7)
-    receive(6)
-    group_jobs(6)
+    group_jobs(6, 4, 13)
     receive(7)
-    jobs(lambda t: (6 - t, 7), 7, "all")
-    jobs(lambda t: (7, t), 8, "end")
+
+    def finish_near(i, o0, o1):
+        if i is None:
+            emit_single(0, o0)
+        else:
+            emit_pair(3 - i, o0, o1)
+
+    jobs(lambda t: (6 - t, 7), 7, finish_near)
+    jobs(lambda t: (7, t), 7)
+    jobs(lambda t: (7, 7), 1, lambda i, o0, o1: emit_single(4, o0))
 
     for way in range(2):
         y_send(way, 1).wait_recv()
@@ -351,30 +393,40 @@
     cross_send(1).wait_recv()
     core_send(y_far, 1).start()
 
-    def out_take(i, c):
-        src = lax.rem(p + i, 16)
-        n = 2 * (2 * lax.rem(src, 8) + src // 8)
-        for j in range(2):
-            here = attn.at[n // 2, j]
-            remote(ostage.at[0, 0], here, os.at[0], orr.at[n + j], f, src).wait_recv()
-        return c
-
-    lax.fori_loop(1, 16, out_take, 0)
-    for h in range(HEADS):
-        at32[HEAD * h : HEAD * h + HEAD, :] = jnp.concatenate(
-            [attn[h, 0, 0:HEAD, :], attn[h, 1, 0:HEAD, :]], axis=1
-        ).astype(F32)
-    for j in range(9):
-        proj[:, 128 * j : 128 * j + 128] = at32[128 * j : 128 * j + 128, :].T.astype(BF16)
-
     for at_y in (y, y_prev, y_next, y_far):
         for kind in range(2):
             n = chip_of(at_y, kind)
             block = rows(1 - core, n, 0, 144)
             remote(block, block, ws.at[9 + n], wr.at[9 + n], other_core, p).wait_recv()
 
-    r = jnp.dot(proj[...], w[0, :, 0:D], preferred_element_type=F32)
-    mid[...] = (hid[...].astype(F32) + mod[2:3] * r).astype(BF16)
+    for h in range(HEADS):
+        at = HEAD * h // 16 * 16
+        off = HEAD * h - at
+        wo[h] = to_rows(w[0, at : at + ROWS, 0:D].astype(F32)[off : off + HEAD])
+    acc_t[...] = jnp.zeros_like(acc_t)
+
+    def out_take(i, c):
+        d = jnp.where(i < 12, 3 - i // 4, jnp.where(i < 14, 0, 4))
+        odd = jnp.where(i < 12, lax.rem(i, 4) // 2, lax.rem(i, 2))
+        lo = jnp.where(odd == 1, 1 - x_lo, x_lo)
+        zs_at = lax.rem(z + jnp.where(lax.rem(i, 2) == 1, d, 8 - d), 8)
+        h = 2 * zs_at + lo
+
+        @pl.when(i != 12)
+        def _():
+            remote(
+                ostage.at[0, 0], attn.at[h], os.at[0], orr.at[h], f, lo * 8 + zs_at
+            ).wait_recv()
+
+        block = attn[h].astype(F32)
+        block = jnp.concatenate([block[0:HEAD], block[HEAD : 2 * HEAD]], axis=1)
+        block = jnp.concatenate([block, jnp.zeros((128 - HEAD, TOK), F32)], axis=0)
+        x = block.T.astype(BF16)
+        acc_t[...] += jnp.dot(x[:, 0:ROWS], wo[h], preferred_element_type=F32)
+        return c
+
+    lax.fori_loop(0, 16, out_take, 0)
+    mid[...] = (hid[...].astype(F32) + mod[2:3] * acc_t[...]).astype(BF16)
 
     def rows16(ref, n):
         return ref.at[pl.ds(pl.multiple_of(16 * n, 16), 16)]
@@ -400,11 +452,11 @@
     lax.fori_loop(1, 8, sel_sent, 0)
     sel_copy(wsel, other_core, f).wait_send()
 
-    def out_sent(n, c):
-        remote(ostage.at[0, 0], attn.at[0, 0], os.at[n], orr.at[0], f, x_pair).wait_send()
-        return c
-
-    lax.fori_loop(2, 32, out_sent, 0)
+    for d in range(5):
+        for odd in range(2):
+            for half in range(2 if 0 < d < 4 else 1):
+                if d + odd > 0:
+                    out_copy(d, odd, half).wait_send()
     for way in range(2):
         cross_send(way).wait_send()
         y_pass(way).wait_send()
@@ -469,22 +521,25 @@
 VMEM = pl.BlockSpec(memory_space=pltpu.VMEM)
 
 
-def block_call(hid, mod, wsel, wrest):
+def block_call(*args):
     dma = pltpu.SemaphoreType.DMA
     return pl.pallas_call(
         block_kernel,
         out_shape=jax.ShapeDtypeStruct((TOK, D), BF16),
-        in_specs=[VMEM] * 4,
+        in_specs=[VMEM] * 6,
         out_specs=VMEM,
         scratch_shapes=[
             pltpu.VMEM((8, TOK, D), BF16),
+            pltpu.VMEM((ROWS, 512), BF16),
+            pltpu.VMEM((2, ROWS, HALF), BF16),
+            pltpu.VMEM((HEADS, ROWS, D), BF16),
             pltpu.VMEM((16, ROWS, 512), BF16),
             pltpu.VMEM((D, 512), BF16),
             pltpu.VMEM((16, 3 * ROWS, TOK), BF16),
             pltpu.VMEM((8, 3 * ROWS, TOK), BF16),
             pltpu.VMEM((4096, 128), BF16),
-            pltpu.VMEM((8, 4, ROWS, 128), BF16),
-            pltpu.VMEM((HEADS, 2, ROWS, 128), BF16),
+            pltpu.VMEM((5, 4, 2 * HEAD, 128), BF16),
+            pltpu.VMEM((HEADS, 2 * HEAD, 128), BF16),
             pltpu.VMEM((ROWS, HALF), BF16),
             pltpu.VMEM((2, D, HALF), BF16),
             pltpu.VMEM((2 * TOK, 2 * TOK), F32),
@@ -493,7 +548,6 @@
             pltpu.VMEM((8, 2 * TOK), F32),
             pltpu.VMEM((8, 1, 2 * TOK), F32),
             pltpu.VMEM((8, ROWS, 2 * TOK), F32),
-            pltpu.VMEM((D, TOK), F32),
             pltpu.VMEM((TOK, D), BF16),
             pltpu.VMEM((TOK, D), BF16),
             pltpu.VMEM((TOK, D), BF16),
@@ -503,7 +557,7 @@
             dma((16,)), dma((16,)),
             dma((16,)), dma((16,)),
             dma((8,)), dma((8,)),
-            dma((32,)), dma((32,)),
+            dma((20,)), dma((16,)),
             dma((17,)), dma((17,)),
             dma((16,)), dma((16,)),
             dma((16,)), dma((16,)),
@@ -512,22 +566,18 @@
             collective_id=0, has_side_effects=True, vmem_limit_bytes=60 * 1024 * 1024
         ),
         name="block",
-    )(hid, mod, wsel, wrest)
+    )(*args)
 
 
 def body(hidden_states, modulation, w_qkv_spatial, w_out_spatial, w_qkv_temporal, w_out_temporal):
-    p = lax.axis_index("patch")
-    z = lax.rem(p, 8)
-    hid = hidden_states.reshape(TOK, D)
-    parts = [
-        lax.dynamic_slice_in_dim(w_qkv_spatial, D * part + 2 * HEAD * z, 2 * HEAD, axis=1)
-        for part in range(3)
-    ]
-    wsel = jnp.pad(jnp.concatenate(parts, axis=1), ((0, ROWS - HEAD), (0, 512 - 6 * HEAD)))
-    rest = jnp.concatenate([w_out_spatial, w_qkv_temporal, w_out_temporal], axis=1)
-    rest = jnp.pad(rest, ((0, ROWS - HEAD), (0, 2 * HALF - 5 * D)))
-    rest = jnp.stack([rest[:, :HALF], rest[:, HALF:]])
-    out = block_call(hid, modulation, wsel, rest)
+    out = block_call(
+        hidden_states.reshape(TOK, D),
+        modulation,
+        w_qkv_spatial,
+        w_out_spatial,
+        w_qkv_temporal,
+        w_out_temporal,
+    )
     return out.reshape(1, TOK, D)
 
 

time: 114 us -> 112 us (0.982)
  other arithmetic: 2.99 us -> 0 us
  Pallas kernels: 108 us -> 110 us
    concatenate x2 -> x0, other arithmetic: 1.95 us -> none  [the longest x1 1.21 us: body(): jnp.concatenate([w_out_spatial, w_qkv_temporal, w_out_temporal], axis=1)]
    pallas_call x1, Pallas kernels: 108 us -> 110 us  [block_call(): pl.pallas_call(block_kernel, out_shape=jax.ShapeDtypeStruct((TOK, D), BF1...]
where the time goes in v4:
time: 112 us
  Pallas kernels  110 us (98%)
  local copies, waits for them, and re-layouts  1.92 us (2%)
    pallas_call x1, Pallas kernels, block_call(): pl.pallas_call(block_kernel, out_shape=jax.ShapeDtypeStruct((TOK, D), BF1...  110 us

profile of v4, /device:TPU:1, one launch (start us, length us, event | category | flops | bytes accessed | tf_op | source)
XLA Modules:
  0.0 111.8 jit_solution(6325541785390171238)
XLA Ops:
  0.0 109.9 %block.1 = bf16[256,1152]{1,0:T(8,128)(2,1)} custom-call(bf16[256,1152]{1,0:T(8,128)(2,1)} %bitcast.3, f32[6,1152]{1,0:T(8,128)} %mod.1, bf16[72,3456]{1,0:T(8,128)(2,1)} %w_qkv_s.1, bf16[72,1152]{1,0:T(8,128)(2,1)} %w_out_s.1, bf16[72,3456]{1,0:T(8,128)(2,1)} %w_qkv_t.1, bf16[72,1152]{1,0:T(8,128)(2,1)} %w_out_t.1), custom_call_target="tpu_custom_call" | custom-call | tf_op jit(solution)/shard_map/block/pallas_call | solution.py:526
  109.9 1.9 %copy.8 = bf16[1,256,1152]{2,1,0:T(8,128)(2,1)} copy(bf16[1,256,1152]{2,1,0:T(8,128)(2,1)} %bitcast.2) | data formatting | bytes 1179648

commit v5 on v4

--- a/solution.py
+++ b/solution.py
@@ -13,6 +13,7 @@
 TOK = 256
 ROWS = 80
 HALF = 2944
+EARLY = 640
 Q_SCALE = HEAD ** (-0.5) * math.log2(math.e)
 F32 = jnp.float32
 BF16 = jnp.bfloat16
@@ -43,7 +44,7 @@
 
 def block_kernel(
     hid, mod, w_qkv_s, w_out_s, w_qkv_t, w_out_t, out,
-    nz, wsel, wrest, wo, wsel_all, wc, qkv, stage, kn, ostage, attn, w1, w, score_a, score_b, top_a, top_b, top_all, acc_all,
+    nz, wsel, wrest, wo, heads, wsel_all, wc, qkv, stage, kn, ostage, attn, w1, w, score_a, score_b, top_a, top_b, top_all, acc_all,
     mid, midt, proj, qkv_t, acc_t, osend,
     zs, zr, ss, sr, xs, xr, os, orr, ws, wr, ms, mr, bs, br,
 ):
@@ -75,29 +76,27 @@
     nz[0] = norm_modulate(hid[...].astype(F32), mod[0:1], mod[1:2]).astype(BF16)
 
     lanes = lax.broadcasted_iota(jnp.int32, (HEAD, TOK), 1)
-    parts = []
+    own, other = [], []
     for part in range(3):
         at = pl.ds(pl.multiple_of(D * part + 128 * z, 128), TOK)
         window = w_qkv_s[:, at].astype(F32)
-        window = pltpu.roll(window, lax.rem(TOK - 16 * z + 16 * part, TOK), axis=1)
-        inside = (lanes >= 16 * part) & (lanes < 16 * part + 2 * HEAD)
-        parts.append(jnp.where(inside, window, 0.0))
-    q, k, v = parts
-    sel = jnp.concatenate(
-        [q[:, 0:128], q[:, 128:] + k[:, 0:128], k[:, 128:] + v[:, 0:128], v[:, 128:]], axis=1
-    )
+        inside = (lanes >= HEAD * part) & (lanes < HEAD * part + HEAD)
+        for which, found in ((x_lo, own), (1 - x_lo, other)):
+            shift = lax.rem(2 * TOK - 16 * z - HEAD * which + HEAD * part, TOK)
+            found.append(jnp.where(inside, pltpu.roll(window, shift, axis=1), 0.0))
+    sel = jnp.concatenate([own[0] + own[1] + own[2], other[0] + other[1] + other[2]], axis=1)
 
     def to_rows(value):
         tail = jnp.zeros((ROWS - HEAD, value.shape[1]), F32)
         return jnp.concatenate([value.astype(F32), tail], axis=0).astype(BF16)
 
     wsel[...] = to_rows(sel)
-    cut = HALF - D
-    wrest[0, :, 0:D] = to_rows(w_out_s[...])
-    wrest[0, :, D:HALF] = to_rows(w_qkv_t[:, 0:cut])
-    wrest[1, :, 0 : 3 * D - cut] = to_rows(w_qkv_t[:, cut:])
-    wrest[1, :, 3 * D - cut : 4 * D - cut] = to_rows(w_out_t[...])
-    wrest[1, :, 4 * D - cut :] = jnp.zeros((ROWS, HALF - 4 * D + cut), BF16)
+    wrest[0, :, 0:EARLY] = to_rows(w_out_s[:, 0:EARLY])
+    wrest[0, :, EARLY:HALF] = to_rows(w_qkv_t[:, 0 : 2 * D])
+    wrest[1, :, 0 : D - EARLY] = to_rows(w_out_s[:, EARLY:D])
+    wrest[1, :, D - EARLY : EARLY] = jnp.zeros((ROWS, 2 * EARLY - D), BF16)
+    wrest[1, :, EARLY : EARLY + D] = to_rows(w_qkv_t[:, 2 * D : 3 * D])
+    wrest[1, :, EARLY + D : HALF] = to_rows(w_out_t[...])
     pl.semaphore_wait(barrier, 31)
 
     def z_block(g, way):
@@ -154,39 +153,83 @@
     def chip_of(at_y, kind):
         return 2 * at_y + (x_hi if kind == 0 else 1 - x_hi)
 
-    def rows(half, n, start, size):
-        return w.at[half, pl.ds(pl.multiple_of(144 * n + start, 16), size)]
+    def rows(half, n, start, size, part):
+        at = pl.ds(pl.multiple_of(144 * n + start, 16), size)
+        return w.at[half, at, pl.ds(EARLY * part, HALF - EARLY if part else EARLY)]
 
     y_prev = lax.rem(y + 3, 4)
     y_next = lax.rem(y + 1, 4)
     y_far = lax.rem(y + 2, 4)
 
-    def cross_send(far):
-        block = rows(core, chip_of(y_far if far else y, 0), 0, 144)
-        return remote(block, block, ws.at[1 + far], wr.at[1 + far], cross_f, x_pair)
-
-    def y_send(way, kind):
-        n = 3 + way * 2 + kind
-        block = rows(core, chip_of(y, kind), 0, 144)
-        return remote(block, block, ws.at[n], wr.at[n], y_dn if way else y_up, p)
-
-    def y_pass(way):
-        block = rows(core, chip_of(y_next if way else y_prev, 0), 80 * way, 64 if way else 80)
-        return remote(block, block, ws.at[7 + way], wr.at[7 + way], y_dn if way else y_up, p)
-
-    def core_send(at_y, kind):
+    def weight_copy(block, n, part, to_f, to_p):
+        n = n + 17 * part
+        return remote(block, block, ws.at[n], wr.at[n], to_f, to_p)
+
+    def cross_send(far, part):
+        block = rows(core, chip_of(y_far if far else y, 0), 0, 144, part)
+        return weight_copy(block, 1 + far, part, cross_f, x_pair)
+
+    def y_send(way, kind, part):
+        block = rows(core, chip_of(y, kind), 0, 144, part)
+        return weight_copy(block, 3 + way * 2 + kind, part, y_dn if way else y_up, p)
+
+    def y_pass(way, part):
+        n = chip_of(y_next if way else y_prev, 0)
+        block = rows(core, n, 80 * way, 64 if way else 80, part)
+        return weight_copy(block, 7 + way, part, y_dn if way else y_up, p)
+
+    def y_pass_in(way, part):
+        block = rows(core, chip_of(y_far, 0), 80 * way, 64 if way else 80, part)
+        return weight_copy(block, 7 + way, part, other_core, p)
+
+    def core_send(at_y, kind, part):
         n = chip_of(at_y, kind)
-        block = rows(core, n, 0, 144)
-        return remote(block, block, ws.at[9 + n], wr.at[9 + n], other_core, p)
-
-    cross_send(0).start()
-    for way in range(2):
-        y_send(way, 0).start()
-    core_send(y, 0).start()
+        return weight_copy(rows(core, n, 0, 144, part), 9 + n, part, other_core, p)
+
+    def core_in(at_y, kind, part):
+        n = chip_of(at_y, kind)
+        return weight_copy(rows(1 - core, n, 0, 144, part), 9 + n, part, other_core, p)
+
+    def near_rows(part):
+        cross_send(0, part).wait_recv()
+        for way in range(2):
+            y_send(way, 0, part).wait_recv()
+            y_pass(way, part).start()
+        for way in range(2):
+            y_send(way, 1, part).start()
+        core_send(y, 1, part).start()
+        core_send(y_prev, 0, part).start()
+        core_send(y_next, 0, part).start()
+
+    def far_rows(part):
+        for way in range(2):
+            y_pass_in(way, part).wait_recv()
+        cross_send(1, part).start()
+        core_send(y_far, 0, part).start()
+
+    def crossed_rows(part):
+        for way in range(2):
+            y_send(way, 1, part).wait_recv()
+        core_send(y_prev, 1, part).start()
+        core_send(y_next, 1, part).start()
+
+    def last_rows(part):
+        cross_send(1, part).wait_recv()
+        core_send(y_far, 1, part).start()
+
+    def all_rows(part):
+        for at_y in (y, y_prev, y_next, y_far):
+            for kind in range(2):
+                core_in(at_y, kind, part).wait_recv()
+
+    for part in range(2):
+        cross_send(0, part).start()
+        for way in range(2):
+            y_send(way, 0, part).start()
+        core_send(y, 0, part).start()
 
     zero8 = jnp.zeros((8, TOK), F32)
     ones8 = jnp.where(lax.broadcasted_iota(jnp.int32, (8, TOK), 0) == 0, 1.0, 0.0)
-    lower = x_lo == 0
 
     def to_natural(slot):
         kt = qkv[slot, ROWS : 2 * ROWS, :].astype(F32)
@@ -197,19 +240,16 @@
         return remote(stage.at[g], qkv.at[2 * g + 1], xs.at[g], xr.at[g], f, x_pair)
 
     def project(g):
-        r = jnp.dot(nz[g], wc[...], preferred_element_type=F32)
-        t = r.T
-        own, oth = [], []
-        for part in range(3):
-            one = t[144 * part : 144 * part + 72]
-            two = t[144 * part + 72 : 144 * part + 144]
-            if part == 0:
-                one, two = one * Q_SCALE, two * Q_SCALE
-            own += [jnp.where(lower, one, two), ones8 if part == 2 else zero8]
-            oth += [jnp.where(lower, two, one), ones8 if part == 2 else zero8]
-        stage[g] = jnp.concatenate(oth, axis=0).astype(BF16)
-        pair_copy(g).start()
-        qkv[2 * g] = jnp.concatenate(own, axis=0).astype(BF16)
+        for lane in (256, 0):
+            r = jnp.dot(nz[g], wc[:, lane : lane + 256], preferred_element_type=F32)
+            t = r.T
+            block = [t[0:72] * Q_SCALE, zero8, t[72:144], zero8, t[144:216], ones8]
+            block = jnp.concatenate(block, axis=0).astype(BF16)
+            if lane:
+                stage[g] = block
+                pair_copy(g).start()
+            else:
+                qkv[2 * g] = block
         to_natural(2 * g)
 
     def receive(g):
@@ -339,40 +379,32 @@
     group_jobs(0, 0, 1)
     group_jobs(1, 0, 3)
     arrive(3)
+    near_rows(0)
     project(3)
     receive(2)
     group_jobs(2, 0, 5)
     arrive(4)
-    cross_send(0).wait_recv()
-    for way in range(2):
-        y_send(way, 0).wait_recv()
-        y_pass(way).start()
-    for way in range(2):
-        y_send(way, 1).start()
-    core_send(y, 1).start()
-    core_send(y_prev, 0).start()
-    core_send(y_next, 0).start()
+    near_rows(1)
     project(4)
     receive(3)
     group_jobs(3, 0, 7)
     arrive(5)
+    far_rows(0)
     project(5)
     receive(4)
     group_jobs(4, 0, 9)
     receive(5)
     group_jobs(5, 0, 4)
     arrive(6)
+    crossed_rows(0)
     project(6)
     group_jobs(5, 4, 11)
-    far = [rows(core, chip_of(y_far, 0), 80 * way, 64 if way else 80) for way in range(2)]
-    for way in range(2):
-        remote(far[way], far[way], ws.at[7 + way], wr.at[7 + way], other_core, p).wait_recv()
-    cross_send(1).start()
-    core_send(y_far, 0).start()
+    far_rows(1)
     receive(6)
     group_jobs(6, 0, 4)
     arrive(7)
     project(7)
+    last_rows(0)
     group_jobs(6, 4, 13)
     receive(7)
 
@@ -386,47 +418,52 @@
     jobs(lambda t: (7, t), 7)
     jobs(lambda t: (7, 7), 1, lambda i, o0, o1: emit_single(4, o0))
 
-    for way in range(2):
-        y_send(way, 1).wait_recv()
-    core_send(y_prev, 1).start()
-    core_send(y_next, 1).start()
-    cross_send(1).wait_recv()
-    core_send(y_far, 1).start()
-
-    for at_y in (y, y_prev, y_next, y_far):
-        for kind in range(2):
-            n = chip_of(at_y, kind)
-            block = rows(1 - core, n, 0, 144)
-            remote(block, block, ws.at[9 + n], wr.at[9 + n], other_core, p).wait_recv()
-
-    for h in range(HEADS):
-        at = HEAD * h // 16 * 16
-        off = HEAD * h - at
-        wo[h] = to_rows(w[0, at : at + ROWS, 0:D].astype(F32)[off : off + HEAD])
-    acc_t[...] = jnp.zeros_like(acc_t)
-
-    def out_take(i, c):
+    all_rows(0)
+    crossed_rows(1)
+
+    def source(i):
         d = jnp.where(i < 12, 3 - i // 4, jnp.where(i < 14, 0, 4))
         odd = jnp.where(i < 12, lax.rem(i, 4) // 2, lax.rem(i, 2))
         lo = jnp.where(odd == 1, 1 - x_lo, x_lo)
-        zs_at = lax.rem(z + jnp.where(lax.rem(i, 2) == 1, d, 8 - d), 8)
-        h = 2 * zs_at + lo
+        at_z = lax.rem(z + jnp.where(lax.rem(i, 2) == 1, d, 8 - d), 8)
+        return lo, at_z
+
+    def lay_out(i, c):
+        lo, at_z = source(i)
+        first = HEAD * (2 * at_z + lo)
+        from_row = first // 16 * 16
+        shifted = first > from_row
+        for half, lane, size in ((0, 0, EARLY), (1, EARLY, D - EARLY)):
+            block = w[half, pl.ds(pl.multiple_of(from_row, 16), ROWS), 0:size].astype(F32)
+            block = jnp.where(shifted, block[ROWS - HEAD :], block[:HEAD])
+            block = jnp.concatenate([block, jnp.zeros((128 - HEAD, size), F32)], axis=0)
+            to = pl.ds(pl.multiple_of(128 * i, 128), 128)
+            wo[to, lane : lane + size] = block.astype(BF16)
+        return c
+
+    lax.fori_loop(0, HEADS, lay_out, 0)
+
+    def out_take(i, c):
+        lo, at_z = source(i)
+        h = 2 * at_z + lo
 
         @pl.when(i != 12)
         def _():
             remote(
-                ostage.at[0, 0], attn.at[h], os.at[0], orr.at[h], f, lo * 8 + zs_at
+                ostage.at[0, 0], attn.at[h], os.at[0], orr.at[h], f, lo * 8 + at_z
             ).wait_recv()
 
         block = attn[h].astype(F32)
         block = jnp.concatenate([block[0:HEAD], block[HEAD : 2 * HEAD]], axis=1)
         block = jnp.concatenate([block, jnp.zeros((128 - HEAD, TOK), F32)], axis=0)
-        x = block.T.astype(BF16)
-        acc_t[...] += jnp.dot(x[:, 0:ROWS], wo[h], preferred_element_type=F32)
-        return c
-
-    lax.fori_loop(0, 16, out_take, 0)
-    mid[...] = (hid[...].astype(F32) + mod[2:3] * acc_t[...]).astype(BF16)
+        heads[:, pl.ds(pl.multiple_of(128 * i, 128), 128)] = block.T.astype(BF16)
+        return c
+
+    lax.fori_loop(0, 12, out_take, 0)
+    acc_t[...] = jnp.dot(heads[:, 0:1536], wo[0:1536, :], preferred_element_type=F32)
+    lax.fori_loop(12, 16, out_take, 0)
+    r = jnp.dot(heads[:, 1536:2048], wo[1536:2048, :], preferred_element_type=F32)
+    mid[...] = (hid[...].astype(F32) + mod[2:3] * (acc_t[...] + r)).astype(BF16)
 
     def rows16(ref, n):
         return ref.at[pl.ds(pl.multiple_of(16 * n, 16), 16)]
@@ -457,14 +494,17 @@
             for half in range(2 if 0 < d < 4 else 1):
                 if d + odd > 0:
                     out_copy(d, odd, half).wait_send()
-    for way in range(2):
-        cross_send(way).wait_send()
-        y_pass(way).wait_send()
-        for kind in range(2):
-            y_send(way, kind).wait_send()
-    for at_y in (y, y_prev, y_next, y_far):
-        for kind in range(2):
-            core_send(at_y, kind).wait_send()
+    last_rows(1)
+    for part in range(2):
+        for way in range(2):
+            cross_send(way, part).wait_send()
+            y_pass(way, part).wait_send()
+            for kind in range(2):
+                y_send(way, kind, part).wait_send()
+        for at_y in (y, y_prev, y_next, y_far):
+            for kind in range(2):
+                core_send(at_y, kind, part).wait_send()
+    all_rows(1)
 
     def take_mid(i, c):
         peer = lax.rem(f + i, 16)
@@ -473,11 +513,11 @@
 
     lax.fori_loop(1, 16, take_mid, 0)
     proj[...] = norm_modulate(midt[...].astype(F32), mod[3:4], mod[4:5]).astype(BF16)
-    a = jnp.dot(proj[...], w[0, :, D:HALF], preferred_element_type=F32)
+    a = jnp.dot(proj[...], w[0, :, EARLY:HALF], preferred_element_type=F32)
     qkv_t[:, 0:D] = (a[:, 0:D] * Q_SCALE).astype(BF16)
-    qkv_t[:, D : HALF - D] = a[:, D:].astype(BF16)
-    b = jnp.dot(proj[...], w[1, :, 0 : 4 * D - HALF], preferred_element_type=F32)
-    qkv_t[:, HALF - D : 3 * D] = b.astype(BF16)
+    qkv_t[:, D : 2 * D] = a[:, D:].astype(BF16)
+    b = jnp.dot(proj[...], w[1, :, EARLY : EARLY + D], preferred_element_type=F32)
+    qkv_t[:, 2 * D :] = b.astype(BF16)
 
     ri = lax.broadcasted_iota(jnp.int32, (TOK, TOK), 0)
     ci = lax.broadcasted_iota(jnp.int32, (TOK, TOK), 1)
@@ -497,9 +537,7 @@
         total = jnp.sum(prob, axis=1, keepdims=True)
         o = jnp.dot(prob.astype(BF16), v, preferred_element_type=F32) / total
         acc_t[:, start : start + 256] = jnp.where(inside, o, acc_t[:, start : start + 256])
-    r = jnp.dot(
-        acc_t[...].astype(BF16), w[1, :, 4 * D - HALF : 5 * D - HALF], preferred_element_type=F32
-    )
+    r = jnp.dot(acc_t[...].astype(BF16), w[1, :, EARLY + D : HALF], preferred_element_type=F32)
     osend[...] = (midt[...].astype(F32) + mod[5:6] * r).astype(BF16)
 
     def send_out(i, c):
@@ -532,7 +570,8 @@
             pltpu.VMEM((8, TOK, D), BF16),
             pltpu.VMEM((ROWS, 512), BF16),
             pltpu.VMEM((2, ROWS, HALF), BF16),
-            pltpu.VMEM((HEADS, ROWS, D), BF16),
+            pltpu.VMEM((HEADS * 128, D), BF16),
+            pltpu.VMEM((TOK, HEADS * 128), BF16),
             pltpu.VMEM((16, ROWS, 512), BF16),
             pltpu.VMEM((D, 512), BF16),
             pltpu.VMEM((16, 3 * ROWS, TOK), BF16),
@@ -558,7 +597,7 @@
             dma((16,)), dma((16,)),
             dma((8,)), dma((8,)),
             dma((20,)), dma((16,)),
-            dma((17,)), dma((17,)),
+            dma((34,)), dma((34,)),
             dma((16,)), dma((16,)),
             dma((16,)), dma((16,)),
         ],

time: 112 us -> 108 us (0.964)
  Pallas kernels: 110 us -> 105 us
    pallas_call x1, Pallas kernels: 110 us -> 105 us  [block_call(): pl.pallas_call(block_kernel, out_shape=jax.ShapeDtypeStruct((TOK, D), BF1...]
where the time goes in v5:
time: 108 us; the launch traced here: 107 us
  Pallas kernels  105 us (97%)
  local copies, waits for them, and re-layouts  1.92 us (2%)
    pallas_call x1, Pallas kernels, block_call(): pl.pallas_call(block_kernel, out_shape=jax.ShapeDtypeStruct((TOK, D), BF1...  105 us

profile of v5, /device:TPU:1, one launch (start us, length us, event | category | flops | bytes accessed | tf_op | source)
XLA Modules:
  0.0 107.4 jit_solution(15373167054556483447)
XLA Ops:
  0.0 105.5 %block.1 = bf16[256,1152]{1,0:T(8,128)(2,1)} custom-call(bf16[256,1152]{1,0:T(8,128)(2,1)} %bitcast.3, f32[6,1152]{1,0:T(8,128)} %mod.1, bf16[72,3456]{1,0:T(8,128)(2,1)} %w_qkv_s.1, bf16[72,1152]{1,0:T(8,128)(2,1)} %w_out_s.1, bf16[72,3456]{1,0:T(8,128)(2,1)} %w_qkv_t.1, bf16[72,1152]{1,0:T(8,128)(2,1)} %w_out_t.1), custom_call_target="tpu_custom_call" | custom-call | tf_op jit(solution)/shard_map/block/pallas_call | solution.py:564
  105.5 1.9 %copy.8 = bf16[1,256,1152]{2,1,0:T(8,128)(2,1)} copy(bf16[1,256,1152]{2,1,0:T(8,128)(2,1)} %bitcast.2) | data formatting | bytes 1179648

commit v6 on v5

--- a/solution.py
+++ b/solution.py
@@ -45,7 +45,7 @@
 def block_kernel(
     hid, mod, w_qkv_s, w_out_s, w_qkv_t, w_out_t, out,
     nz, wsel, wrest, wo, heads, wsel_all, wc, qkv, stage, kn, ostage, attn, w1, w, score_a, score_b, top_a, top_b, top_all, acc_all,
-    mid, midt, proj, qkv_t, acc_t, osend,
+    midp, midt, qkv_t, acc_t, osend, outp,
     zs, zr, ss, sr, xs, xr, os, orr, ws, wr, ms, mr, bs, br,
 ):
     f = lax.axis_index("frame")
@@ -262,29 +262,29 @@
     top_all[...] = jnp.full(top_all.shape, -1e30, F32)
     acc_all[...] = jnp.zeros(acc_all.shape, F32)
 
-    def out_copy(d, odd, half):
-        to = (1 - x_lo if odd else x_lo) * 8 + lax.rem(z + (d if half else 8 - d), 8)
+    def out_copy(g, odd, half):
+        s = (g + 1) // 2
+        if isinstance(g, int):
+            batch = half if g in (0, 7) else (g + 1) % 2
+        else:
+            batch = lax.rem(g + 1, 2)
+        to = (1 - x_lo if odd else x_lo) * 8 + lax.rem(z + (s if half else 8 - s), 8)
         n = 2 * odd + half
-        return remote(ostage.at[d, n], attn.at[head], os.at[4 * d + n], orr.at[head], f, to)
-
-    def emit(d, odd, half, first_rows, last_rows):
-        n = 2 * odd + half
-        ostage[d, n] = jnp.concatenate([first_rows, last_rows], axis=0).astype(BF16)
-        if isinstance(d, int) and d == 0 and odd == 0:
-            attn[head] = ostage[d, n]
-        else:
-            out_copy(d, odd, half).start()
-
-    def emit_single(d, o):
-        for odd in range(2):
-            at = 256 * odd
-            emit(d, odd, 0, o[:, at : at + 128], o[:, at + 128 : at + 256])
-
-    def emit_pair(d, o0, o1):
+        return remote(
+            ostage.at[g, n], attn.at[head, batch], os.at[4 * g + n], orr.at[2 * head + batch], f, to
+        )
+
+    def emit(g, o):
+        both = isinstance(g, int) and g in (0, 7)
+        o = jnp.concatenate([o, jnp.zeros((8, 2 * TOK), F32)], axis=0).astype(BF16)
         for odd in range(2):
             for half in range(2):
-                at = 128 * (2 * odd + half)
-                emit(d, odd, half, o0[:, at : at + 128], o1[:, at : at + 128])
+                n = 2 * odd + half
+                ostage[g, n] = o[:, 128 * n : 128 * n + 128]
+                if both and g + odd == 0:
+                    attn[head, half] = ostage[g, n]
+                elif not (both and half):
+                    out_copy(g, odd, half).start()
 
     def score_steps(gq, gk, buf):
         q_t = jnp.concatenate([qkv[2 * gq, 0:ROWS, :], qkv[2 * gq + 1, 0:ROWS, :]], axis=1)
@@ -318,26 +318,26 @@
         top_all[gq] = m
         acc_all[gq] = acc
 
-    def jobs(pick, count, finish=None):
-        last = finish is not None
+    def jobs(pick, count, finish=False):
         for step in score_steps(*pick(0), 0):
             step()
         rest = 1 if count % 2 else 2
 
+        def one(at, buf, following):
+            o = job(*at, buf, following, finish)
+            if finish:
+                emit(at[0], o)
+
         def two(i, c):
-            o1 = job(*pick(2 * i), 0, pick(2 * i + 1), last)
-            o0 = job(*pick(2 * i + 1), 1, pick(2 * i + 2), last)
-            if last:
-                finish(i, o0, o1)
+            one(pick(2 * i), 0, pick(2 * i + 1))
+            one(pick(2 * i + 1), 1, pick(2 * i + 2))
             return c
 
         if count > rest:
             lax.fori_loop(0, (count - rest) // 2, two, 0)
         for t in range(count - rest, count):
             following = pick(t + 1) if t + 1 < count else None
-            o = job(*pick(t), (t - count + rest) % 2, following, last)
-        if last:
-            finish(None, o, None)
+            one(pick(t), (t - count + rest) % 2, following)
 
     def group_jobs(g, begin, end):
         def pick(t):
@@ -408,15 +408,12 @@
     group_jobs(6, 4, 13)
     receive(7)
 
-    def finish_near(i, o0, o1):
-        if i is None:
-            emit_single(0, o0)
-        else:
-            emit_pair(3 - i, o0, o1)
-
-    jobs(lambda t: (6 - t, 7), 7, finish_near)
+    jobs(lambda t: (0 if isinstance(t, int) and t == 3 else 5 - 2 * t, 7), 4, True)
     jobs(lambda t: (7, t), 7)
-    jobs(lambda t: (7, 7), 1, lambda i, o0, o1: emit_single(4, o0))
+    jobs(lambda t: (7, 7), 1, True)
+    for g, odd in ((7, 0), (7, 1), (0, 1)):
+        out_copy(g, odd, 1).start()
+    jobs(lambda t: (6 - 2 * t, 7), 3, True)
 
     all_rows(0)
     crossed_rows(1)
@@ -443,39 +440,63 @@
 
     lax.fori_loop(0, HEADS, lay_out, 0)
 
-    def out_take(i, c):
-        lo, at_z = source(i)
-        h = 2 * at_z + lo
-
-        @pl.when(i != 12)
-        def _():
-            remote(
-                ostage.at[0, 0], attn.at[h], os.at[0], orr.at[h], f, lo * 8 + at_z
-            ).wait_recv()
-
-        block = attn[h].astype(F32)
-        block = jnp.concatenate([block[0:HEAD], block[HEAD : 2 * HEAD]], axis=1)
-        block = jnp.concatenate([block, jnp.zeros((128 - HEAD, TOK), F32)], axis=0)
-        heads[:, pl.ds(pl.multiple_of(128 * i, 128), 128)] = block.T.astype(BF16)
-        return c
-
-    lax.fori_loop(0, 12, out_take, 0)
-    acc_t[...] = jnp.dot(heads[:, 0:1536], wo[0:1536, :], preferred_element_type=F32)
-    lax.fori_loop(12, 16, out_take, 0)
-    r = jnp.dot(heads[:, 1536:2048], wo[1536:2048, :], preferred_element_type=F32)
-    mid[...] = (hid[...].astype(F32) + mod[2:3] * (acc_t[...] + r)).astype(BF16)
-
     def rows16(ref, n):
         return ref.at[pl.ds(pl.multiple_of(16 * n, 16), 16)]
 
-    def send_mid(i, c):
-        peer = lax.rem(f + i, 16)
-        remote(rows16(mid, peer), rows16(midt, f), ms.at[i], mr.at[f], peer, p).start()
-        return c
-
-    lax.fori_loop(1, 16, send_mid, 0)
-    here = pl.ds(pl.multiple_of(16 * f, 16), 16)
-    midt[here, :] = mid[here, :]
+    def pack(value):
+        rest = jnp.concatenate([value[:, EARLY:], jnp.zeros((128, 2 * EARLY - D), F32)], axis=1)
+        sides = [value[:, :EARLY].reshape(16, 8, EARLY), rest.reshape(16, 8, EARLY)]
+        return jnp.concatenate(sides, axis=1).reshape(TOK, EARLY).astype(BF16)
+
+    def unpack(ref):
+        value = ref[...].astype(F32).reshape(16, 16, EARLY)
+        return jnp.concatenate([value[:, 0:8], value[:, 8:16, 0 : D - EARLY]], axis=2).reshape(128, D)
+
+    def swap_start(source, target, ssem, rsem, b):
+        def send(i, c):
+            peer = lax.rem(f + i, 16)
+            remote(
+                rows16(source.at[b], peer), rows16(target.at[b], f),
+                ssem.at[16 * b + i], rsem.at[16 * b + f], peer, p,
+            ).start()
+            return c
+
+        lax.fori_loop(1, 16, send, 0)
+        here = pl.ds(pl.multiple_of(16 * f, 16), 16)
+        target[b, here, :] = source[b, here, :]
+
+    def swap_wait(source, target, ssem, rsem, b):
+        def take(i, c):
+            peer = lax.rem(f + i, 16)
+            remote(
+                rows16(source.at[b], peer), rows16(target.at[b], peer),
+                ssem.at[16 * b + i], rsem.at[16 * b + peer], peer, p,
+            ).wait()
+            return c
+
+        lax.fori_loop(1, 16, take, 0)
+
+    for b in range(2):
+        def out_take(i, c, b=b):
+            lo, at_z = source(i)
+            h = 2 * at_z + lo
+
+            @pl.when(i != 12)
+            def _():
+                remote(
+                    ostage.at[0, 0], attn.at[h, b], os.at[0], orr.at[2 * h + b], f, lo * 8 + at_z
+                ).wait_recv()
+
+            block = attn[h, b].astype(F32)
+            block = jnp.concatenate([block, jnp.zeros((128 - ROWS, 128), F32)], axis=0)
+            heads[:, pl.ds(pl.multiple_of(128 * i, 128), 128)] = block.T.astype(BF16)
+            return c
+
+        lax.fori_loop(0, HEADS, out_take, 0)
+        r = jnp.dot(heads[...], wo[...], preferred_element_type=F32)
+        mid = hid[128 * b : 128 * b + 128, :].astype(F32) + mod[2:3] * r
+        midp[b] = pack(mid)
+        swap_start(midp, midt, ms, mr, b)
 
     for g in range(1, 8):
         for way in range(2):
@@ -488,12 +509,11 @@
 
     lax.fori_loop(1, 8, sel_sent, 0)
     sel_copy(wsel, other_core, f).wait_send()
-
-    for d in range(5):
+    for g in range(8):
         for odd in range(2):
-            for half in range(2 if 0 < d < 4 else 1):
-                if d + odd > 0:
-                    out_copy(d, odd, half).wait_send()
+            for half in range(2):
+                if g + odd > 0:
+                    out_copy(g, odd, half).wait_send()
     last_rows(1)
     for part in range(2):
         for way in range(2):
@@ -506,54 +526,40 @@
                 core_send(at_y, kind, part).wait_send()
     all_rows(1)
 
-    def take_mid(i, c):
-        peer = lax.rem(f + i, 16)
-        remote(rows16(mid, peer), rows16(midt, peer), ms.at[i], mr.at[peer], peer, p).wait()
-        return c
-
-    lax.fori_loop(1, 16, take_mid, 0)
-    proj[...] = norm_modulate(midt[...].astype(F32), mod[3:4], mod[4:5]).astype(BF16)
-    a = jnp.dot(proj[...], w[0, :, EARLY:HALF], preferred_element_type=F32)
-    qkv_t[:, 0:D] = (a[:, 0:D] * Q_SCALE).astype(BF16)
-    qkv_t[:, D : 2 * D] = a[:, D:].astype(BF16)
-    b = jnp.dot(proj[...], w[1, :, EARLY : EARLY + D], preferred_element_type=F32)
-    qkv_t[:, 2 * D :] = b.astype(BF16)
-
-    ri = lax.broadcasted_iota(jnp.int32, (TOK, TOK), 0)
-    ci = lax.broadcasted_iota(jnp.int32, (TOK, TOK), 1)
-    same = lax.rem(ri, 16) == lax.rem(ci, 16)
-    acc_t[...] = jnp.zeros_like(acc_t)
-    for h in range(HEADS):
-        start = 128 * min(HEAD * h // 128, 7)
-        low = HEAD * h - start
-        inside = (ci >= low) & (ci < low + HEAD)
-        q = qkv_t[:, start : start + 256]
-        q = jnp.where(inside, q, jnp.zeros_like(q))
-        k = qkv_t[:, D + start : D + start + 256]
-        v = qkv_t[:, 2 * D + start : 2 * D + start + 256]
-        s = lax.dot_general(q, k, (((1,), (1,)), ((), ())), preferred_element_type=F32)
-        s = jnp.where(same, s, -1e30)
-        prob = jnp.exp2(s - jnp.max(s, axis=1, keepdims=True))
-        total = jnp.sum(prob, axis=1, keepdims=True)
-        o = jnp.dot(prob.astype(BF16), v, preferred_element_type=F32) / total
-        acc_t[:, start : start + 256] = jnp.where(inside, o, acc_t[:, start : start + 256])
-    r = jnp.dot(acc_t[...].astype(BF16), w[1, :, EARLY + D : HALF], preferred_element_type=F32)
-    osend[...] = (midt[...].astype(F32) + mod[5:6] * r).astype(BF16)
-
-    def send_out(i, c):
-        peer = lax.rem(f + i, 16)
-        remote(rows16(osend, peer), rows16(out, f), bs.at[i], br.at[f], peer, p).start()
-        return c
-
-    lax.fori_loop(1, 16, send_out, 0)
-    out[here, :] = osend[here, :]
-
-    def take_out(i, c):
-        peer = lax.rem(f + i, 16)
-        remote(rows16(osend, peer), rows16(out, peer), bs.at[i], br.at[peer], peer, p).wait()
-        return c
-
-    lax.fori_loop(1, 16, take_out, 0)
+    ri = lax.broadcasted_iota(jnp.int32, (128, 128), 0)
+    ci = lax.broadcasted_iota(jnp.int32, (128, 128), 1)
+    same = lax.rem(ri, 8) == lax.rem(ci, 8)
+    lane = lax.broadcasted_iota(jnp.int32, (128, TOK), 1)
+    for b in range(2):
+        swap_wait(midp, midt, ms, mr, b)
+        value = unpack(midt.at[b])
+        normed = norm_modulate(value, mod[3:4], mod[4:5]).astype(BF16)
+        r = jnp.dot(normed, w[0, :, EARLY:HALF], preferred_element_type=F32)
+        qkv_t[:, 0:D] = (r[:, 0:D] * Q_SCALE).astype(BF16)
+        qkv_t[:, D : 2 * D] = r[:, D:].astype(BF16)
+        r = jnp.dot(normed, w[1, :, EARLY : EARLY + D], preferred_element_type=F32)
+        qkv_t[:, 2 * D :] = r.astype(BF16)
+        acc_t[...] = jnp.zeros_like(acc_t)
+        for h in range(HEADS):
+            start = 128 * min(HEAD * h // 128, 7)
+            low = HEAD * h - start
+            inside = (lane >= low) & (lane < low + HEAD)
+            q = qkv_t[:, start : start + 256]
+            q = jnp.where(inside, q, jnp.zeros_like(q))
+            k = qkv_t[:, D + start : D + start + 256]
+            v = qkv_t[:, 2 * D + start : 2 * D + start + 256]
+            s = lax.dot_general(q, k, (((1,), (1,)), ((), ())), preferred_element_type=F32)
+            s = jnp.where(same, s, -1e30)
+            prob = jnp.exp2(s - jnp.max(s, axis=1, keepdims=True))
+            total = jnp.sum(prob, axis=1, keepdims=True)
+            o = jnp.dot(prob.astype(BF16), v, preferred_element_type=F32) / total
+            acc_t[:, start : start + 256] = jnp.where(inside, o, acc_t[:, start : start + 256])
+        r = jnp.dot(acc_t[...].astype(BF16), w[1, :, EARLY + D : HALF], preferred_element_type=F32)
+        osend[b] = pack(unpack(midt.at[b]) + mod[5:6] * r)
+        swap_start(osend, outp, bs, br, b)
+    for b in range(2):
+        swap_wait(osend, outp, bs, br, b)
+        out[128 * b : 128 * b + 128, :] = unpack(outp.at[b]).astype(BF16)
 
 
 VMEM = pl.BlockSpec(memory_space=pltpu.VMEM)
@@ -571,14 +577,14 @@
             pltpu.VMEM((ROWS, 512), BF16),
             pltpu.VMEM((2, ROWS, HALF), BF16),
             pltpu.VMEM((HEADS * 128, D), BF16),
-            pltpu.VMEM((TOK, HEADS * 128), BF16),
+            pltpu.VMEM((128, HEADS * 128), BF16),
             pltpu.VMEM((16, ROWS, 512), BF16),
             pltpu.VMEM((D, 512), BF16),
             pltpu.VMEM((16, 3 * ROWS, TOK), BF16),
             pltpu.VMEM((8, 3 * ROWS, TOK), BF16),
             pltpu.VMEM((4096, 128), BF16),
-            pltpu.VMEM((5, 4, 2 * HEAD, 128), BF16),
-            pltpu.VMEM((HEADS, 2 * HEAD, 128), BF16),
+            pltpu.VMEM((8, 4, ROWS, 128), BF16),
+            pltpu.VMEM((HEADS, 2, ROWS, 128), BF16),
             pltpu.VMEM((ROWS, HALF), BF16),
             pltpu.VMEM((2, D, HALF), BF16),
             pltpu.VMEM((2 * TOK, 2 * TOK), F32),
@@ -587,19 +593,19 @@
             pltpu.VMEM((8, 2 * TOK), F32),
             pltpu.VMEM((8, 1, 2 * TOK), F32),
             pltpu.VMEM((8, ROWS, 2 * TOK), F32),
-            pltpu.VMEM((TOK, D), BF16),
-            pltpu.VMEM((TOK, D), BF16),
-            pltpu.VMEM((TOK, D), BF16),
-            pltpu.VMEM((TOK, 3 * D), BF16),
-            pltpu.VMEM((TOK, D), F32),
-            pltpu.VMEM((TOK, D), BF16),
+            pltpu.VMEM((2, TOK, EARLY), BF16),
+            pltpu.VMEM((2, TOK, EARLY), BF16),
+            pltpu.VMEM((128, 3 * D), BF16),
+            pltpu.VMEM((128, D), F32),
+            pltpu.VMEM((2, TOK, EARLY), BF16),
+            pltpu.VMEM((2, TOK, EARLY), BF16),
             dma((16,)), dma((16,)),
             dma((16,)), dma((16,)),
             dma((8,)), dma((8,)),
-            dma((20,)), dma((16,)),
+            dma((32,)), dma((32,)),
             dma((34,)), dma((34,)),
-            dma((16,)), dma((16,)),
-            dma((16,)), dma((16,)),
+            dma((32,)), dma((32,)),
+            dma((32,)), dma((32,)),
         ],
         compiler_params=pltpu.CompilerParams(
             collective_id=0, has_side_effects=True, vmem_limit_bytes=60 * 1024 * 1024

time: 108 us -> 104 us (0.963)
  Pallas kernels: 105 us -> 102 us
    pallas_call x1, Pallas kernels: 105 us -> 102 us  [block_call(): pl.pallas_call(block_kernel, out_shape=jax.ShapeDtypeStruct((TOK, D), BF1...]
where the time goes in v6:
time: 104 us
  Pallas kernels  102 us (98%)
  local copies, waits for them, and re-layouts  1.92 us (2%)
    pallas_call x1, Pallas kernels, block_call(): pl.pallas_call(block_kernel, out_shape=jax.ShapeDtypeStruct((TOK, D), BF1...  102 us

profile of v6, /device:TPU:1, one launch (start us, length us, event | category | flops | bytes accessed | tf_op | source)
XLA Modules:
  0.0 103.9 jit_solution(9861328807693559649)
XLA Ops:
  0.0 102.0 %block.1 = bf16[256,1152]{1,0:T(8,128)(2,1)} custom-call(bf16[256,1152]{1,0:T(8,128)(2,1)} %bitcast.3, f32[6,1152]{1,0:T(8,128)} %mod.1, bf16[72,3456]{1,0:T(8,128)(2,1)} %w_qkv_s.1, bf16[72,1152]{1,0:T(8,128)(2,1)} %w_out_s.1, bf16[72,3456]{1,0:T(8,128)(2,1)} %w_qkv_t.1, bf16[72,1152]{1,0:T(8,128)(2,1)} %w_out_t.1), custom_call_target="tpu_custom_call" | custom-call | tf_op jit(solution)/shard_map/block/pallas_call | solution.py:570
  102.0 1.9 %copy.8 = bf16[1,256,1152]{2,1,0:T(8,128)(2,1)} copy(bf16[1,256,1152]{2,1,0:T(8,128)(2,1)} %bitcast.2) | data formatting | bytes 1179648

commit v7 on v6

--- a/solution.py
+++ b/solution.py
@@ -45,8 +45,8 @@
 def block_kernel(
     hid, mod, w_qkv_s, w_out_s, w_qkv_t, w_out_t, out,
     nz, wsel, wrest, wo, heads, wsel_all, wc, qkv, stage, kn, ostage, attn, w1, w, score_a, score_b, top_a, top_b, top_all, acc_all,
-    midp, midt, qkv_t, acc_t, osend, outp,
-    zs, zr, ss, sr, xs, xr, os, orr, ws, wr, ms, mr, bs, br,
+    midp, midt, qkv_t, acc_t, osend, outp, done,
+    zs, zr, ss, sr, xs, xr, os, orr, ws, wr, ms, mr, bs, br, ls,
 ):
     f = lax.axis_index("frame")
     p = lax.axis_index("patch")
@@ -66,12 +66,9 @@
 
     barrier = pltpu.get_barrier_semaphore()
 
-    def greet(i, c):
+    for i in range(1, 16):
+        signal(barrier, f, lax.rem(p + i, 16))
         signal(barrier, lax.rem(f + i, 16), p)
-        signal(barrier, f, lax.rem(p + i, 16))
-        return c
-
-    lax.fori_loop(1, 16, greet, 0)
     signal(barrier, cross_f, x_pair)
     nz[0] = norm_modulate(hid[...].astype(F32), mod[0:1], mod[1:2]).astype(BF16)
 
@@ -236,8 +233,10 @@
         kt = jnp.concatenate([kt, jnp.zeros((128 - ROWS, TOK), F32)], axis=0)
         kn[slot * TOK : slot * TOK + TOK, :] = kt.T.astype(BF16)
 
-    def pair_copy(g):
-        return remote(stage.at[g], qkv.at[2 * g + 1], xs.at[g], xr.at[g], f, x_pair)
+    def pair_copy(g, start=0, size=3 * ROWS):
+        n = 8 if g == 7 and start == 0 else g
+        at = pl.ds(start, size)
+        return remote(stage.at[g, at], qkv.at[2 * g + 1, at], xs.at[n], xr.at[n], f, x_pair)
 
     def project(g):
         for lane in (256, 0):
@@ -247,13 +246,20 @@
             block = jnp.concatenate(block, axis=0).astype(BF16)
             if lane:
                 stage[g] = block
-                pair_copy(g).start()
+                if g == 7:
+                    pair_copy(g, ROWS, 2 * ROWS).start()
+                    pair_copy(g, 0, ROWS).start()
+                else:
+                    pair_copy(g).start()
             else:
                 qkv[2 * g] = block
         to_natural(2 * g)
 
     def receive(g):
-        pair_copy(g).wait()
+        if g == 7:
+            pair_copy(g, ROWS, 2 * ROWS).wait()
+        else:
+            pair_copy(g).wait()
         to_natural(2 * g + 1)
 
     head = 2 * z + x_lo
@@ -409,6 +415,7 @@
     receive(7)
 
     jobs(lambda t: (0 if isinstance(t, int) and t == 3 else 5 - 2 * t, 7), 4, True)
+    pair_copy(7, 0, ROWS).wait()
     jobs(lambda t: (7, t), 7)
     jobs(lambda t: (7, 7), 1, True)
     for g, odd in ((7, 0), (7, 1), (0, 1)):
@@ -452,29 +459,30 @@
         value = ref[...].astype(F32).reshape(16, 16, EARLY)
         return jnp.concatenate([value[:, 0:8], value[:, 8:16, 0 : D - EARLY]], axis=2).reshape(128, D)
 
+    steps = [(j // 4, j // 2 % 2, j % 2) for j in range(1, 16)]
+    steps.sort(key=lambda j: -(min(j[0], 4 - j[0]) + 2 * j[1]))
+
+    def swap_peer(n):
+        dy, dx, dc = steps[n]
+        at_x = 1 - x_hi if dx else x_hi
+        return lax.rem(y + dy, 4) * 4 + at_x * 2 + (1 - core if dc else core)
+
+    def swap_copy(source, target, ssem, rsem, b, n, to, at):
+        return remote(
+            rows16(source.at[b], to), rows16(target.at[b], at),
+            ssem.at[16 * b + n], rsem.at[16 * b + at], to, p,
+        )
+
     def swap_start(source, target, ssem, rsem, b):
-        def send(i, c):
-            peer = lax.rem(f + i, 16)
-            remote(
-                rows16(source.at[b], peer), rows16(target.at[b], f),
-                ssem.at[16 * b + i], rsem.at[16 * b + f], peer, p,
-            ).start()
-            return c
-
-        lax.fori_loop(1, 16, send, 0)
+        for n in range(15):
+            swap_copy(source, target, ssem, rsem, b, n, swap_peer(n), f).start()
         here = pl.ds(pl.multiple_of(16 * f, 16), 16)
         target[b, here, :] = source[b, here, :]
 
     def swap_wait(source, target, ssem, rsem, b):
-        def take(i, c):
-            peer = lax.rem(f + i, 16)
-            remote(
-                rows16(source.at[b], peer), rows16(target.at[b], peer),
-                ssem.at[16 * b + i], rsem.at[16 * b + peer], peer, p,
-            ).wait()
-            return c
-
-        lax.fori_loop(1, 16, take, 0)
+        for n in range(15):
+            peer = swap_peer(n)
+            swap_copy(source, target, ssem, rsem, b, n, peer, peer).wait()
 
     for b in range(2):
         def out_take(i, c, b=b):
@@ -557,9 +565,17 @@
         r = jnp.dot(acc_t[...].astype(BF16), w[1, :, EARLY + D : HALF], preferred_element_type=F32)
         osend[b] = pack(unpack(midt.at[b]) + mod[5:6] * r)
         swap_start(osend, outp, bs, br, b)
+
+    def leave(b):
+        at = pl.ds(128 * b, 128)
+        return pltpu.make_async_copy(done.at[at], out.at[at], ls.at[b])
+
     for b in range(2):
         swap_wait(osend, outp, bs, br, b)
-        out[128 * b : 128 * b + 128, :] = unpack(outp.at[b]).astype(BF16)
+        done[128 * b : 128 * b + 128, :] = unpack(outp.at[b]).astype(BF16)
+        leave(b).start()
+    for b in range(2):
+        leave(b).wait()
 
 
 VMEM = pl.BlockSpec(memory_space=pltpu.VMEM)
@@ -571,7 +587,7 @@
         block_kernel,
         out_shape=jax.ShapeDtypeStruct((TOK, D), BF16),
         in_specs=[VMEM] * 6,
-        out_specs=VMEM,
+        out_specs=pl.BlockSpec(memory_space=pl.ANY),
         scratch_shapes=[
             pltpu.VMEM((8, TOK, D), BF16),
             pltpu.VMEM((ROWS, 512), BF16),
@@ -599,13 +615,15 @@
             pltpu.VMEM((128, D), F32),
             pltpu.VMEM((2, TOK, EARLY), BF16),
             pltpu.VMEM((2, TOK, EARLY), BF16),
+            pltpu.VMEM((TOK, D), BF16),
             dma((16,)), dma((16,)),
             dma((16,)), dma((16,)),
-            dma((8,)), dma((8,)),
+            dma((9,)), dma((9,)),
             dma((32,)), dma((32,)),
             dma((34,)), dma((34,)),
             dma((32,)), dma((32,)),
             dma((32,)), dma((32,)),
+            dma((2,)),
         ],
         compiler_params=pltpu.CompilerParams(
             collective_id=0, has_side_effects=True, vmem_limit_bytes=60 * 1024 * 1024

time: 104 us -> 104 us (level)
  no operation moved by 1% of the time
where the time goes in v7:
time: 104 us
  Pallas kernels  102 us (98%)
  local copies, waits for them, and re-layouts  1.92 us (2%)
    pallas_call x1, Pallas kernels, block_call(): pl.pallas_call(block_kernel, out_shape=jax.ShapeDtypeStruct((TOK, D), BF1...  102 us

profile of v7, /device:TPU:1, one launch (start us, length us, event | category | flops | bytes accessed | tf_op | source)
XLA Modules:
  0.0 103.7 jit_solution(4513670952107563471)
XLA Ops:
  0.0 101.8 %block.1 = bf16[256,1152]{1,0:T(8,128)(2,1)} custom-call(bf16[256,1152]{1,0:T(8,128)(2,1)} %bitcast.3, f32[6,1152]{1,0:T(8,128)} %mod.1, bf16[72,3456]{1,0:T(8,128)(2,1)} %w_qkv_s.1, bf16[72,1152]{1,0:T(8,128)(2,1)} %w_out_s.1, bf16[72,3456]{1,0:T(8,128)(2,1)} %w_qkv_t.1, bf16[72,1152]{1,0:T(8,128)(2,1)} %w_out_t.1), custom_call_target="tpu_custom_call" | custom-call | tf_op jit(solution)/shard_map/block/pallas_call | solution.py:586
  101.8 1.9 %copy.8 = bf16[1,256,1152]{2,1,0:T(8,128)(2,1)} copy(bf16[1,256,1152]{2,1,0:T(8,128)(2,1)} %bitcast.2) | data formatting | bytes 1179648

commit v8 on v7

--- a/solution.py
+++ b/solution.py
@@ -45,7 +45,7 @@
 def block_kernel(
     hid, mod, w_qkv_s, w_out_s, w_qkv_t, w_out_t, out,
     nz, wsel, wrest, wo, heads, wsel_all, wc, qkv, stage, kn, ostage, attn, w1, w, score_a, score_b, top_a, top_b, top_all, acc_all,
-    midp, midt, qkv_t, acc_t, osend, outp, done,
+    midp, midt, qkv_t, acc_t, osend,
     zs, zr, ss, sr, xs, xr, os, orr, ws, wr, ms, mr, bs, br, ls,
 ):
     f = lax.axis_index("frame")
@@ -70,7 +70,41 @@
         signal(barrier, f, lax.rem(p + i, 16))
         signal(barrier, lax.rem(f + i, 16), p)
     signal(barrier, cross_f, x_pair)
-    nz[0] = norm_modulate(hid[...].astype(F32), mod[0:1], mod[1:2]).astype(BF16)
+
+    def norm_rows(at):
+        value = norm_modulate(hid[at : at + 128, :].astype(F32), mod[0:1], mod[1:2])
+        nz[0, at : at + 128, :] = value.astype(BF16)
+
+    norm_rows(0)
+
+    pl.semaphore_wait(barrier, 31)
+
+    def z_block(g, way):
+        return nz.at[g, pl.ds(128 * way, 128)]
+
+    def z_hop(g, way):
+        if g <= 2:
+            source = nz.at[0, pl.ds(128 * (g - 1), 128)]
+        elif g <= 6:
+            source = z_block(g - 2, way)
+        else:
+            source = z_block(5 + way, way)
+        n = 2 * g + way
+        return remote(source, z_block(g, way), zs.at[n], zr.at[n], f, z_dn if way else z_up)
+
+    for g in (1, 2):
+        if g == 2:
+            norm_rows(128)
+        for way in range(2):
+            z_hop(g, way).start()
+
+    def arrive(g):
+        for way in range(2):
+            z_hop(g, way).wait_recv()
+            if g <= 4:
+                z_hop(g + 2, way).start()
+            elif g == 5 + way:
+                z_hop(7, way).start()
 
     lanes = lax.broadcasted_iota(jnp.int32, (HEAD, TOK), 1)
     own, other = [], []
@@ -88,54 +122,28 @@
         return jnp.concatenate([value.astype(F32), tail], axis=0).astype(BF16)
 
     wsel[...] = to_rows(sel)
+    def sel_copy(source, peer, n):
+        return remote(source, wsel_all.at[n], ss.at[n], sr.at[n], peer, p)
+
+    sel_copy(wsel, other_core, f).start()
+
+    def sel_send(i, c):
+        peer = lax.rem(f + 2 * i, 16)
+        remote(wsel, wsel_all.at[f], ss.at[peer], sr.at[f], peer, p).start()
+        return c
+
+    lax.fori_loop(1, 8, sel_send, 0)
+    wsel_all[f] = wsel[...]
+
     wrest[0, :, 0:EARLY] = to_rows(w_out_s[:, 0:EARLY])
     wrest[0, :, EARLY:HALF] = to_rows(w_qkv_t[:, 0 : 2 * D])
     wrest[1, :, 0 : D - EARLY] = to_rows(w_out_s[:, EARLY:D])
     wrest[1, :, D - EARLY : EARLY] = jnp.zeros((ROWS, 2 * EARLY - D), BF16)
     wrest[1, :, EARLY : EARLY + D] = to_rows(w_qkv_t[:, 2 * D : 3 * D])
     wrest[1, :, EARLY + D : HALF] = to_rows(w_out_t[...])
-    pl.semaphore_wait(barrier, 31)
-
-    def z_block(g, way):
-        return nz.at[g, pl.ds(128 * way, 128)]
-
-    def z_hop(g, way):
-        if g <= 2:
-            source = nz.at[0, pl.ds(128 * (g - 1), 128)]
-        elif g <= 6:
-            source = z_block(g - 2, way)
-        else:
-            source = z_block(5 + way, way)
-        n = 2 * g + way
-        return remote(source, z_block(g, way), zs.at[n], zr.at[n], f, z_dn if way else z_up)
-
-    for g in (1, 2):
-        for way in range(2):
-            z_hop(g, way).start()
-
-    def arrive(g):
-        for way in range(2):
-            z_hop(g, way).wait_recv()
-            if g <= 4:
-                z_hop(g + 2, way).start()
-            elif g == 5 + way:
-                z_hop(7, way).start()
-
     first = remote(wrest.at[1 - core], w1, ws.at[0], wr.at[0], other_core, p)
     first.start()
 
-    def sel_copy(source, peer, n):
-        return remote(source, wsel_all.at[n], ss.at[n], sr.at[n], peer, p)
-
-    sel_copy(wsel, other_core, f).start()
-
-    def sel_send(i, c):
-        peer = lax.rem(f + 2 * i, 16)
-        remote(wsel, wsel_all.at[f], ss.at[peer], sr.at[f], peer, p).start()
-        return c
-
-    lax.fori_loop(1, 8, sel_send, 0)
-    wsel_all[f] = wsel[...]
 
     first.wait()
     mine = wrest[core, 0:72, :].astype(F32)
@@ -455,10 +463,6 @@
         sides = [value[:, :EARLY].reshape(16, 8, EARLY), rest.reshape(16, 8, EARLY)]
         return jnp.concatenate(sides, axis=1).reshape(TOK, EARLY).astype(BF16)
 
-    def unpack(ref):
-        value = ref[...].astype(F32).reshape(16, 16, EARLY)
-        return jnp.concatenate([value[:, 0:8], value[:, 8:16, 0 : D - EARLY]], axis=2).reshape(128, D)
-
     steps = [(j // 4, j // 2 % 2, j % 2) for j in range(1, 16)]
     steps.sort(key=lambda j: -(min(j[0], 4 - j[0]) + 2 * j[1]))
 
@@ -476,8 +480,6 @@
     def swap_start(source, target, ssem, rsem, b):
         for n in range(15):
             swap_copy(source, target, ssem, rsem, b, n, swap_peer(n), f).start()
-        here = pl.ds(pl.multiple_of(16 * f, 16), 16)
-        target[b, here, :] = source[b, here, :]
 
     def swap_wait(source, target, ssem, rsem, b):
         for n in range(15):
@@ -505,6 +507,8 @@
         mid = hid[128 * b : 128 * b + 128, :].astype(F32) + mod[2:3] * r
         midp[b] = pack(mid)
         swap_start(midp, midt, ms, mr, b)
+        here = pl.ds(pl.multiple_of(16 * f, 16), 16)
+        midt[b, here, :] = midp[b, here, :]
 
     for g in range(1, 8):
         for way in range(2):
@@ -533,6 +537,9 @@
             for kind in range(2):
                 core_send(at_y, kind, part).wait_send()
     all_rows(1)
+
+    def keep(b):
+        return pltpu.make_async_copy(rows16(osend.at[b], f), rows16(out.at[b], f), ls.at[b])
 
     ri = lax.broadcasted_iota(jnp.int32, (128, 128), 0)
     ci = lax.broadcasted_iota(jnp.int32, (128, 128), 1)
@@ -564,18 +571,22 @@
             acc_t[:, start : start + 256] = jnp.where(inside, o, acc_t[:, start : start + 256])
         r = jnp.dot(acc_t[...].astype(BF16), w[1, :, EARLY + D : HALF], preferred_element_type=F32)
         osend[b] = pack(unpack(midt.at[b]) + mod[5:6] * r)
-        swap_start(osend, outp, bs, br, b)
-
-    def leave(b):
-        at = pl.ds(128 * b, 128)
-        return pltpu.make_async_copy(done.at[at], out.at[at], ls.at[b])
+        swap_start(osend, out, bs, br, b)
+        keep(b).start()
 
     for b in range(2):
-        swap_wait(osend, outp, bs, br, b)
-        done[128 * b : 128 * b + 128, :] = unpack(outp.at[b]).astype(BF16)
-        leave(b).start()
+        swap_wait(osend, out, bs, br, b)
+        keep(b).wait()
+
+
+def unpack(ref):
+    value = ref[...].astype(F32).reshape(16, 16, EARLY)
+    return jnp.concatenate([value[:, 0:8], value[:, 8:16, 0 : D - EARLY]], axis=2).reshape(128, D)
+
+
+def unpack_kernel(packed, out):
     for b in range(2):
-        leave(b).wait()
+        out[128 * b : 128 * b + 128, :] = unpack(packed.at[b]).astype(BF16)
 
 
 VMEM = pl.BlockSpec(memory_space=pltpu.VMEM)
@@ -585,7 +596,7 @@
     dma = pltpu.SemaphoreType.DMA
     return pl.pallas_call(
         block_kernel,
-        out_shape=jax.ShapeDtypeStruct((TOK, D), BF16),
+        out_shape=jax.ShapeDtypeStruct((2, TOK, EARLY), BF16),
         in_specs=[VMEM] * 6,
         out_specs=pl.BlockSpec(memory_space=pl.ANY),
         scratch_shapes=[
@@ -614,8 +625,6 @@
             pltpu.VMEM((128, 3 * D), BF16),
             pltpu.VMEM((128, D), F32),
             pltpu.VMEM((2, TOK, EARLY), BF16),
-            pltpu.VMEM((2, TOK, EARLY), BF16),
-            pltpu.VMEM((TOK, D), BF16),
             dma((16,)), dma((16,)),
             dma((16,)), dma((16,)),
             dma((9,)), dma((9,)),
@@ -641,6 +650,13 @@
         w_qkv_temporal,
         w_out_temporal,
     )
+    out = pl.pallas_call(
+        unpack_kernel,
+        out_shape=jax.ShapeDtypeStruct((TOK, D), BF16),
+        in_specs=[VMEM],
+        out_specs=VMEM,
+        name="unpack",
+    )(out)
     return out.reshape(1, TOK, D)
 
 

time: 104 us -> 103 us (level)
  local copies, waits for them, and re-layouts: 1.92 us -> 0 us
    unnamed x1 -> x0, local copies, waits for them, and re-layouts: 1.92 us -> none
    pallas_call x1 -> x2, Pallas kernels: 102 us -> 103 us  [the longest x1 101 us: block_call(): pl.pallas_call(block_kernel, out_shape=jax.ShapeDtypeStruct((2, TOK, EARL...]
where the time goes in v8:
time: 103 us
  Pallas kernels  103 us (100%)
    pallas_call x1, Pallas kernels, block_call(): pl.pallas_call(block_kernel, out_shape=jax.ShapeDtypeStruct((2, TOK, EARL...  101 us

profile of v8, /device:TPU:1, one launch (start us, length us, event | category | flops | bytes accessed | tf_op | source)
XLA Modules:
  0.0 103.0 jit_solution(7463703632807858486)
XLA Ops:
  0.0 101.1 %block.1.packed = bf16[2,256,640]{2,1,0:T(8,128)(2,1)} custom-call(bf16[256,1152]{1,0:T(8,128)(2,1)} %bitcast.2, f32[6,1152]{1,0:T(8,128)} %mod.1, bf16[72,3456]{1,0:T(8,128)(2,1)} %w_qkv_s.1, bf16[72,1152]{1,0:T(8,128)(2,1)} %w_out_s.1, bf16[72,3456]{1,0:T(8,128)(2,1)} %w_qkv_t.1, bf16[72,1152]{1,0:T(8,128)(2,1)} %w_out_t.1), custom_call_target="tpu_custom_call" | custom-call | tf_op jit(solution)/shard_map/block/pallas_call | solution.py:597
  101.1 1.9 %unpack.1 = bf16[256,1152]{1,0:T(8,128)(2,1)} custom-call(bf16[2,256,640]{2,1,0:T(8,128)(2,1)} %block.1.packed), custom_call_target="tpu_custom_call" | custom-call | tf_op jit(solution)/shard_map/unpack/pallas_call | solution.py:653

commit v9 on v8

--- a/solution.py
+++ b/solution.py
@@ -502,8 +502,17 @@
             heads[:, pl.ds(pl.multiple_of(128 * i, 128), 128)] = block.T.astype(BF16)
             return c
 
-        lax.fori_loop(0, HEADS, out_take, 0)
-        r = jnp.dot(heads[...], wo[...], preferred_element_type=F32)
+        late = 8 if b else 12
+        if b:
+            lax.fori_loop(12, HEADS, out_take, 0)
+        lax.fori_loop(0, late, out_take, 0)
+        r = jnp.dot(heads[:, 0 : 128 * late], wo[0 : 128 * late, :], preferred_element_type=F32)
+        if b:
+            r += jnp.dot(heads[:, 1536:], wo[1536:, :], preferred_element_type=F32)
+        acc_t[...] = r
+        lax.fori_loop(late, late + 4, out_take, 0)
+        at = slice(128 * late, 128 * late + 512)
+        r = acc_t[...] + jnp.dot(heads[:, at], wo[at, :], preferred_element_type=F32)
         mid = hid[128 * b : 128 * b + 128, :].astype(F32) + mod[2:3] * r
         midp[b] = pack(mid)
         swap_start(midp, midt, ms, mr, b)

time: 103 us -> 103 us (level)
  no operation moved by 1% of the time
where the time goes in v9:
time: 103 us
  Pallas kernels  103 us (100%)
    pallas_call x1, Pallas kernels, block_call(): pl.pallas_call(block_kernel, out_shape=jax.ShapeDtypeStruct((2, TOK, EARL...  101 us

profile of v9, /device:TPU:1, one launch (start us, length us, event | category | flops | bytes accessed | tf_op | source)
XLA Modules:
  0.0 102.7 jit_solution(9924563818743849796)
XLA Ops:
  0.0 100.7 %block.1.packed = bf16[2,256,640]{2,1,0:T(8,128)(2,1)} custom-call(bf16[256,1152]{1,0:T(8,128)(2,1)} %bitcast.2, f32[6,1152]{1,0:T(8,128)} %mod.1, bf16[72,3456]{1,0:T(8,128)(2,1)} %w_qkv_s.1, bf16[72,1152]{1,0:T(8,128)(2,1)} %w_out_s.1, bf16[72,3456]{1,0:T(8,128)(2,1)} %w_qkv_t.1, bf16[72,1152]{1,0:T(8,128)(2,1)} %w_out_t.1), custom_call_target="tpu_custom_call" | custom-call | tf_op jit(solution)/shard_map/block/pallas_call | solution.py:606
  100.7 1.9 %unpack.1 = bf16[256,1152]{1,0:T(8,128)(2,1)} custom-call(bf16[2,256,640]{2,1,0:T(8,128)(2,1)} %block.1.packed), custom_call_target="tpu_custom_call" | custom-call | tf_op jit(solution)/shard_map/unpack/pallas_call | solution.py:662
